TPU v7x, 32 devices: a whole 2x2x4 slice. The times are simulated.
32 devices in a mesh: dp: 2 (over y), ctx: 4 (over x, core), tensor: 4 (over z).
Axes of the slice: x: 2, y: 2, z: 4, core: 2. Of those that a mesh axis runs over, the one named last changes fastest.
Arguments:
- hidden_in: bfloat16 [2, 2048, 2048], P('dp', 'ctx'), may hold values from -6 to 6
- positions: int32 [2, 2048], P('dp'), may hold values from 0 to 2047, as said below
- cotangent: bfloat16 [2, 2048, 2048], P('dp', 'ctx'), may hold values from -6 to 6
- w_qkv: float32 [2048, 3072], P(('dp', 'ctx'), 'tensor'), may hold values from -0.15625 to 0.15625
- w_qkv_first: float32 [2048, 3072], P(('dp', 'ctx'), 'tensor'), may hold values from -40 to 40
- w_qkv_second: float32 [2048, 3072], P(('dp', 'ctx'), 'tensor'), may hold values from 217.088 to 860.16
- w_out: float32 [2048, 2048], P('tensor', ('dp', 'ctx')), may hold values from -0.75 to 0.75
- w_out_first: float32 [2048, 2048], P('tensor', ('dp', 'ctx')), may hold values from -4 to 4
- w_out_second: float32 [2048, 2048], P('tensor', ('dp', 'ctx')), may hold values from 0.625 to 2.5
- w_gate_up: float32 [2048, 16384], P(('dp', 'ctx'), 'tensor'), may hold values from -0.125 to 0.125
- w_gate_up_first: float32 [2048, 16384], P(('dp', 'ctx'), 'tensor'), may hold values from -12 to 12
- w_gate_up_second: float32 [2048, 16384], P(('dp', 'ctx'), 'tensor'), may hold values from 19.6608 to 77.824
- w_down: float32 [8192, 2048], P('tensor', ('dp', 'ctx')), may hold values from -0.0625 to 0.0625
- w_down_first: float32 [8192, 2048], P('tensor', ('dp', 'ctx')), may hold values from -24 to 24
- w_down_second: float32 [8192, 2048], P('tensor', ('dp', 'ctx')), may hold values from 77.824 to 311.296
- norm_gains: float32 [2, 2048], P(None, ('dp', 'ctx')), may hold values from 0.1 to 1.9
- norm_gains_first: float32 [2, 2048], P(None, ('dp', 'ctx')), may hold values from -40 to 40
- norm_gains_second: float32 [2, 2048], P(None, ('dp', 'ctx')), may hold values from 217.088 to 860.16
Outputs:
- block_out: bfloat16 [2, 2048, 2048], P('dp', 'ctx')
- grad_in: float32 [2, 2048, 2048], P('dp', 'ctx')
- w_qkv_first_new: float32 [2048, 3072], P(('dp', 'ctx'), 'tensor')
- w_qkv_second_new: float32 [2048, 3072], P(('dp', 'ctx'), 'tensor')
- w_qkv_new: float32 [2048, 3072], P(('dp', 'ctx'), 'tensor')
- w_out_first_new: float32 [2048, 2048], P('tensor', ('dp', 'ctx'))
- w_out_second_new: float32 [2048, 2048], P('tensor', ('dp', 'ctx'))
- w_out_new: float32 [2048, 2048], P('tensor', ('dp', 'ctx'))
- w_gate_up_first_new: float32 [2048, 16384], P(('dp', 'ctx'), 'tensor')
- w_gate_up_second_new: float32 [2048, 16384], P(('dp', 'ctx'), 'tensor')
- w_gate_up_new: float32 [2048, 16384], P(('dp', 'ctx'), 'tensor')
- w_down_first_new: float32 [8192, 2048], P('tensor', ('dp', 'ctx'))
- w_down_second_new: float32 [8192, 2048], P('tensor', ('dp', 'ctx'))
- w_down_new: float32 [8192, 2048], P('tensor', ('dp', 'ctx'))
- norm_gains_first_new: float32 [2, 2048], P(None, ('dp', 'ctx'))
- norm_gains_second_new: float32 [2, 2048], P(None, ('dp', 'ctx'))
- norm_gains_new: float32 [2, 2048], P(None, ('dp', 'ctx'))
Inputs may be any that keep to these rules, and one draw needn't show every extreme that they name: Each row is a permutation of the positions of one sequence, made of aligned runs of 256 tokens holding consecutive rising positions, each run starting at a multiple of 256.
All inputs are finite; a program needn't handle non-finite values.
Results may differ from a plain program's by a relative error of at most 0.015.
The roundings to bfloat16 on the way count: a program that leaves them out, or rounds other values in their place, can miss the bound.
Values may be sent and summed in bfloat16 or wider, within the bound.
No kernel may reach another device: no remote copies, remote signals or barrier semaphores. Data moves between devices by JAX's collectives and lax.ppermute only.
A program may use at most 256 MiB of HBM per device.

v0:
```python
import math

import jax
import jax.numpy as jnp
from jax import lax
from jax.sharding import PartitionSpec as P

HQ = 32
KV = 8
HD = 64
FF = 8192
STEP = 10


NORM_EPS = 1e-05
ROPE_THETA = 500000.0
SCORE_SCALE = 0.125
LEARN_RATE = 0.01
OUT_RATE = 0.05
GAIN_RATE = 0.25
BETA_ONE = 0.9
BETA_TWO = 0.95
ADAM_EPS = 1e-08
WEIGHT_DECAY = 0.1


def contract(left, right, left_dim, right_dim):
    return lax.dot_general(
        left, right, (((left_dim,), (right_dim,)), ((), ())), preferred_element_type=jnp.float32
    )


def rotate(vectors, places, flip_sign):
    half = vectors.shape[-1] // 2
    freqs = ROPE_THETA ** (-(jnp.arange(half, dtype=jnp.float32) * 2.0 / vectors.shape[-1]))
    angles = places.astype(jnp.float32)[:, None] * freqs[None, :]
    cosine = jnp.cos(angles)[:, None, :]
    sine = flip_sign * jnp.sin(angles)[:, None, :]
    first = vectors[..., :half]
    second = vectors[..., half:]
    return jnp.concatenate(
        [first * cosine - second * sine, second * cosine + first * sine], axis=-1
    )


def normalize(values):
    factor = lax.rsqrt(jnp.mean(values * values, axis=-1, keepdims=True) + NORM_EPS)
    return (values * factor, factor)


def norm_back(grad_hat, x_hat, factor):
    return factor * (grad_hat - x_hat * jnp.mean(grad_hat * x_hat, axis=-1, keepdims=True))


def adamw_step(weight, first, second, gradient, step_rate, decay_rate):
    first_new = BETA_ONE * first + (1.0 - BETA_ONE) * gradient
    second_new = BETA_TWO * second + (1.0 - BETA_TWO) * gradient * gradient
    first_hat = first_new / (1.0 - BETA_ONE**STEP)
    second_hat = second_new / (1.0 - BETA_TWO**STEP)
    weight_new = weight - step_rate * (
        first_hat / (jnp.sqrt(second_hat) + ADAM_EPS) + decay_rate * weight
    )
    return (first_new, second_new, weight_new)


def block_scores(queries, key_block, place_block, query_places):
    scores = (
        jnp.einsum("qgrd,kgd->grqk", queries, key_block, preferred_element_type=jnp.float32)
        * SCORE_SCALE
    )
    visible = (place_block[None, :] <= query_places[:, None])[None, None]
    return (scores, visible)


def attend_forward(queries, key_blocks, value_blocks, place_blocks, query_places):

    def sweep(running, slices):
        highest, total_sum = running
        key_block, place_block = slices
        scores, visible = block_scores(queries, key_block, place_block, query_places)
        scores = jnp.where(visible, scores, -1e30)
        new_high = jnp.maximum(highest, jnp.max(scores, axis=-1))
        shifted = jnp.where(visible, jnp.exp(scores - new_high[..., None]), 0.0)
        total_sum = total_sum * jnp.exp(highest - new_high) + jnp.sum(shifted, axis=-1)
        return ((new_high, total_sum), None)

    start_high = jnp.full(
        (queries.shape[1], queries.shape[2], queries.shape[0]), -1e30, jnp.float32
    )
    (highest, total_sum), unused = lax.scan(
        sweep, (start_high, jnp.zeros_like(start_high)), (key_blocks, place_blocks)
    )
    log_total = highest + jnp.log(total_sum)

    def collect(summed, slices):
        key_block, value_block, place_block = slices
        scores, visible = block_scores(queries, key_block, place_block, query_places)
        probabilities = jnp.where(visible, jnp.exp(scores - log_total[..., None]), 0.0).astype(
            jnp.bfloat16
        )
        return (
            summed
            + jnp.einsum(
                "grqk,kgd->qgrd", probabilities, value_block, preferred_element_type=jnp.float32
            ),
            None,
        )

    mixed_heads, unused = lax.scan(
        collect, jnp.zeros(queries.shape, jnp.float32), (key_blocks, value_blocks, place_blocks)
    )
    return (mixed_heads, log_total)


def attend_backward(
    queries, key_blocks, value_blocks, place_blocks, query_places, mixed_heads, log_total, d_mixed
):
    row_dot = jnp.transpose(jnp.sum(d_mixed.astype(jnp.float32) * mixed_heads, axis=-1), (1, 2, 0))

    def sweep(d_query, slices):
        key_block, value_block, place_block = slices
        scores, visible = block_scores(queries, key_block, place_block, query_places)
        probabilities = jnp.where(visible, jnp.exp(scores - log_total[..., None]), 0.0)
        d_probs = jnp.einsum(
            "qgrd,kgd->grqk", d_mixed, value_block, preferred_element_type=jnp.float32
        )
        d_scores = (probabilities * (d_probs - row_dot[..., None])).astype(jnp.bfloat16)
        d_query = (
            d_query
            + jnp.einsum("grqk,kgd->qgrd", d_scores, key_block, preferred_element_type=jnp.float32)
            * SCORE_SCALE
        )
        d_keys = (
            jnp.einsum("grqk,qgrd->kgd", d_scores, queries, preferred_element_type=jnp.float32)
            * SCORE_SCALE
        )
        d_values = jnp.einsum(
            "grqk,qgrd->kgd",
            probabilities.astype(jnp.bfloat16),
            d_mixed,
            preferred_element_type=jnp.float32,
        )
        row_count = key_block.shape[0]
        return (
            d_query,
            jnp.concatenate(
                [d_keys.reshape(row_count, -1), d_values.reshape(row_count, -1)], axis=1
            ),
        )

    d_query, kv_terms = lax.scan(
        sweep, jnp.zeros(queries.shape, jnp.float32), (key_blocks, value_blocks, place_blocks)
    )
    return (d_query, kv_terms.reshape(-1, kv_terms.shape[-1]))


def local(
    hidden_in,
    positions,
    cotangent,
    w_qkv,
    w_qkv_first,
    w_qkv_second,
    w_out,
    w_out_first,
    w_out_second,
    w_gate_up,
    w_gate_up_first,
    w_gate_up_second,
    w_down,
    w_down_first,
    w_down_second,
    norm_gains,
    norm_gains_first,
    norm_gains_second,
):
    tensor_count = lax.axis_size("tensor")
    heads_here = HQ // tensor_count
    kv_here = KV // tensor_count
    head_ratio = HQ // KV
    units_here = FF // tensor_count
    q_cols = heads_here * HD
    k_cols = kv_here * HD
    tok_rows = hidden_in.shape[1]
    seq_rows = positions.shape[1]
    place_row = positions[0]
    query_places = lax.dynamic_slice_in_dim(place_row, lax.axis_index("ctx") * tok_rows, tok_rows)
    residual = hidden_in[0].astype(jnp.float32)
    fetched = (
        lax.all_gather(w_qkv.astype(jnp.bfloat16), ("dp", "ctx"), axis=0, tiled=True),
        lax.all_gather(w_out.astype(jnp.bfloat16), ("dp", "ctx"), axis=1, tiled=True),
        lax.all_gather(w_gate_up.astype(jnp.bfloat16), ("dp", "ctx"), axis=0, tiled=True),
        lax.all_gather(w_down.astype(jnp.bfloat16), ("dp", "ctx"), axis=1, tiled=True),
        lax.all_gather(norm_gains.astype(jnp.bfloat16), ("dp", "ctx"), axis=1, tiled=True),
    )
    full_qkv, full_out, full_gate_up, full_down, full_gains = fetched
    gain_values = full_gains.astype(jnp.float32)
    x_hat_one, factor_one = normalize(residual)
    normed_one = (x_hat_one * gain_values[0]).astype(jnp.bfloat16)
    projected = jnp.dot(normed_one, full_qkv, preferred_element_type=jnp.float32)
    queries = rotate(
        projected[:, :q_cols].reshape(tok_rows, heads_here, HD), query_places, 1.0
    ).astype(jnp.bfloat16)
    queries = queries.reshape(tok_rows, kv_here, head_ratio, HD)
    keys_here = rotate(
        projected[:, q_cols : q_cols + k_cols].reshape(tok_rows, kv_here, HD), query_places, 1.0
    ).astype(jnp.bfloat16)
    values_here = projected[:, q_cols + k_cols :].astype(jnp.bfloat16)
    joined = jnp.concatenate([keys_here.reshape(tok_rows, k_cols), values_here], axis=1)
    every_kv = lax.all_gather(joined, "ctx", axis=0, tiled=True)
    block_len = math.gcd(seq_rows, 1024)
    block_count = seq_rows // block_len
    key_blocks = every_kv[:, :k_cols].reshape(block_count, block_len, kv_here, HD)
    value_blocks = every_kv[:, k_cols:].reshape(block_count, block_len, kv_here, HD)
    place_blocks = place_row.reshape(block_count, block_len)
    mixed_heads, log_total = attend_forward(
        queries, key_blocks, value_blocks, place_blocks, query_places
    )
    attn_in = mixed_heads.reshape(tok_rows, q_cols).astype(jnp.bfloat16)
    attn_branch = lax.psum(jnp.dot(attn_in, full_out, preferred_element_type=jnp.float32), "tensor")
    middle = residual + attn_branch
    x_hat_two, factor_two = normalize(middle)
    normed_two = (x_hat_two * gain_values[1]).astype(jnp.bfloat16)
    gate_up = jnp.dot(normed_two, full_gate_up, preferred_element_type=jnp.float32)
    gate_part = gate_up[:, :units_here]
    up_part = gate_up[:, units_here:]
    gate_sigmoid = jax.nn.sigmoid(gate_part)
    activated = (gate_part * gate_sigmoid * up_part).astype(jnp.bfloat16)
    ffn_branch = lax.psum(
        jnp.dot(activated, full_down, preferred_element_type=jnp.float32), "tensor"
    )
    block_out = (middle + ffn_branch).astype(jnp.bfloat16).reshape(hidden_in.shape)
    grad_top = cotangent[0]
    d_act = contract(grad_top, full_down, 1, 1)
    d_gate = d_act * up_part * gate_sigmoid * (1.0 + gate_part * (1.0 - gate_sigmoid))
    d_up = d_act * gate_part * gate_sigmoid
    d_gate_up = jnp.concatenate([d_gate, d_up], axis=1).astype(jnp.bfloat16)
    grad_down = contract(activated, grad_top, 0, 0)
    grad_gate_up = contract(normed_two, d_gate_up, 0, 0)
    d_normed_two = lax.psum(contract(d_gate_up, full_gate_up, 1, 1), "tensor")
    grad_gain_two = jnp.sum(d_normed_two * x_hat_two, axis=0)
    d_middle = grad_top.astype(jnp.float32) + norm_back(
        d_normed_two * gain_values[1], x_hat_two, factor_two
    )
    d_mid_low = d_middle.astype(jnp.bfloat16)
    grad_out = contract(attn_in, d_mid_low, 0, 0)
    d_mixed = (
        contract(d_mid_low, full_out, 1, 1)
        .astype(jnp.bfloat16)
        .reshape(tok_rows, kv_here, head_ratio, HD)
    )
    d_query, kv_terms = attend_backward(
        queries,
        key_blocks,
        value_blocks,
        place_blocks,
        query_places,
        mixed_heads,
        log_total,
        d_mixed,
    )
    d_kv = lax.psum_scatter(kv_terms, "ctx", scatter_dimension=0, tiled=True)
    d_q_raw = rotate(d_query.reshape(tok_rows, heads_here, HD), query_places, -1.0).reshape(
        tok_rows, q_cols
    )
    d_k_raw = rotate(d_kv[:, :k_cols].reshape(tok_rows, kv_here, HD), query_places, -1.0).reshape(
        tok_rows, k_cols
    )
    d_projected = jnp.concatenate([d_q_raw, d_k_raw, d_kv[:, k_cols:]], axis=1).astype(jnp.bfloat16)
    grad_qkv = contract(normed_one, d_projected, 0, 0)
    d_normed_one = lax.psum(contract(d_projected, full_qkv, 1, 1), "tensor")
    grad_gain_one = jnp.sum(d_normed_one * x_hat_one, axis=0)
    grad_in = d_middle + norm_back(d_normed_one * gain_values[0], x_hat_one, factor_one)
    reduced = (
        lax.psum_scatter(grad_qkv, ("dp", "ctx"), scatter_dimension=0, tiled=True),
        lax.psum_scatter(grad_out, ("dp", "ctx"), scatter_dimension=1, tiled=True),
        lax.psum_scatter(grad_gate_up, ("dp", "ctx"), scatter_dimension=0, tiled=True),
        lax.psum_scatter(grad_down, ("dp", "ctx"), scatter_dimension=1, tiled=True),
        lax.psum_scatter(
            jnp.stack([grad_gain_one, grad_gain_two]),
            ("dp", "ctx"),
            scatter_dimension=1,
            tiled=True,
        ),
    )
    red_qkv, red_out, red_gate_up, red_down, red_gains = reduced
    qkv_first, qkv_second, qkv_new = adamw_step(
        w_qkv, w_qkv_first, w_qkv_second, red_qkv, LEARN_RATE, WEIGHT_DECAY
    )
    out_first, out_second, out_new = adamw_step(
        w_out, w_out_first, w_out_second, red_out, OUT_RATE, WEIGHT_DECAY
    )
    gu_first, gu_second, gu_new = adamw_step(
        w_gate_up, w_gate_up_first, w_gate_up_second, red_gate_up, LEARN_RATE, WEIGHT_DECAY
    )
    down_first, down_second, down_new = adamw_step(
        w_down, w_down_first, w_down_second, red_down, LEARN_RATE, WEIGHT_DECAY
    )
    gain_first, gain_second, gain_new = adamw_step(
        norm_gains, norm_gains_first, norm_gains_second, red_gains, GAIN_RATE, 0.0
    )
    return (
        block_out,
        grad_in.reshape(hidden_in.shape),
        qkv_first,
        qkv_second,
        qkv_new,
        out_first,
        out_second,
        out_new,
        gu_first,
        gu_second,
        gu_new,
        down_first,
        down_second,
        down_new,
        gain_first,
        gain_second,
        gain_new,
    )


def solution(mesh):
    placed = (
        P("dp", "ctx", None),
        P("dp", None),
        P("dp", "ctx", None),
        P(("dp", "ctx"), "tensor"),
        P(("dp", "ctx"), "tensor"),
        P(("dp", "ctx"), "tensor"),
        P("tensor", ("dp", "ctx")),
        P("tensor", ("dp", "ctx")),
        P("tensor", ("dp", "ctx")),
        P(("dp", "ctx"), "tensor"),
        P(("dp", "ctx"), "tensor"),
        P(("dp", "ctx"), "tensor"),
        P("tensor", ("dp", "ctx")),
        P("tensor", ("dp", "ctx")),
        P("tensor", ("dp", "ctx")),
        P(None, ("dp", "ctx")),
        P(None, ("dp", "ctx")),
        P(None, ("dp", "ctx")),
    )
    return jax.shard_map(
        local,
        mesh=mesh,
        in_specs=placed,
        out_specs=(
            P("dp", "ctx", None),
            P("dp", "ctx", None),
            P(("dp", "ctx"), "tensor"),
            P(("dp", "ctx"), "tensor"),
            P(("dp", "ctx"), "tensor"),
            P("tensor", ("dp", "ctx")),
            P("tensor", ("dp", "ctx")),
            P("tensor", ("dp", "ctx")),
            P(("dp", "ctx"), "tensor"),
            P(("dp", "ctx"), "tensor"),
            P(("dp", "ctx"), "tensor"),
            P("tensor", ("dp", "ctx")),
            P("tensor", ("dp", "ctx")),
            P("tensor", ("dp", "ctx")),
            P(None, ("dp", "ctx")),
            P(None, ("dp", "ctx")),
            P(None, ("dp", "ctx")),
        ),
        check_vma=False,
    )
```

profile of v0, /device:TPU:0, one launch (start us, length us, event | category | flops | bytes accessed | tf_op | source)
XLA Modules:
  0.0 1536.1 jit_solution(3433220778912334263)
XLA Ops:
  10.6 10.3 all_gather.18
  24.1 21.4 %all-gather.6.cloned.1.call-done = bf16[2048,768]{1,0:T(8,128)(2,1)} async-done(((bf16[256,768]{1,0:T(8,128)(2,1)}), bf16[2048,768]{1,0:T(8,128)(2,1)}) %all-gather.6.cloned.1.call-update) | async-done | bytes 3145744 | tf_op jit(solution)/shard_map/all_gather | solution.py:190
  55.5 12.6 all-gather.8.cloned.1.call-done
  71.6 33.6 %while.37 = (s32[]{:T(128)}, f32[2,4,512]{2,1,0:T(4,128)S(1)}, f32[2,4,512]{2,1,0:T(4,128)S(1)}, s32[2,1024]{1,0:T(2,128)S(1)}, s32[512]{0:T(512)S(1)}, /*index=...) while((s32[]{:T(128)}, f32[2,4,512]{2,1,0:T(4,128)S(1)}, ...), condition=%wide.region_4.5_spmd.clone, body=%wide.region_1.4_spmd.clone.sunk | while | flops 570970112 | bytes 36141172 | solution.py:90
  72.0 8.5 fusion.143
  80.5 7.9 select_reduce_fusion.2
  88.9 8.3 fusion.143
  97.2 8.0 select_reduce_fusion.2
  107.6 14.7 while.38
  136.1 147.7 %all-reduce.5.cloned.1.call-done = f32[512,2048]{1,0:T(8,128)} async-done(((f32[512,2048]{1,0:T(8,128)}), f32[512,2048]{1,0:T(8,128)}) %all-reduce.5.cloned.1.call-update) | async-done | bytes 4194320 | tf_op jit(solution)/shard_map/psum | solution.py:220
  288.6 86.6 %all-gather.12.cloned.1.call-done = bf16[2048,4096]{1,0:T(8,128)(2,1)} async-done(((bf16[256,4096]{1,0:T(8,128)(2,1)}), bf16[2048,4096]{1,0:T(8,128)(2,1)}) %all-gather.12.cloned.1.call-update) | async-done | bytes 16777232 | tf_op jit(solution)/shard_map/all_gather | solution.py:192
  375.2 15.7 %fusion.89 = f32[512,4096]{1,0:T(8,128)} fusion(bf16[2048,4096]{1,0:T(8,128)(2,1)} %all-gather.12.cloned.1.call-done, f32[512,2048]{1,0:T(8,128)} %get-tuple-element.399, f32[2048]{0:T(1024)S(1)} %bitcast.251, f32[512]{0:T(512)S(1)} %add_rsqrt_fusion), kind=kOutput, calls=%fused_computation.152 | convolution fusion | flops 8593080320 | bytes 29370368 | tf_op jit(solution)/shard_map/dot_general | solution.py:224
  390.9 42.7 %all-gather.14.cloned.1.call-done = bf16[2048,2048]{1,0:T(8,128)(2,1)} async-done(((bf16[2048,256]{1,0:T(8,128)(2,1)}), bf16[2048,2048]{1,0:T(8,128)(2,1)}) %all-gather.14.cloned.1.call-update) | async-done | bytes 8388624 | tf_op jit(solution)/shard_map/all_gather | solution.py:193
  433.6 11.9 multiply_convert_fusion.1
  447.6 13.8 fusion.67
  461.6 154.9 %all-reduce.7.cloned.1.call-done = f32[512,2048]{1,0:T(8,128)} async-done(((f32[512,2048]{1,0:T(8,128)}), f32[512,2048]{1,0:T(8,128)}) %all-reduce.7.cloned.1.call-update) | async-done | bytes 4194320 | tf_op jit(solution)/shard_map/psum | solution.py:240
  627.1 70.2 %while.39 = (s32[]{:T(128)}, f32[512,2,4,64]{0,3,2,1:T(8,128)}, f32[2,1024,256]{2,1,0:T(8,128)}, bf16[2,1024,2,64]{1,3,2,0:T(8,128)(2,1)}, s32[2,1024]{1,0:T(2,1...) while((s32[]{:T(128)}, f32[512,2,4,64]{0,3,2,1:T(8,128)}, ...), condition=%wide.region_14.15_spmd.clone, body=%wide.region_13.14_spmd.clone.sunk | while | flops 2728001536 | bytes 156694768 | solution.py:151
  631.4 9.4 fusion.161
  666.4 9.4 fusion.161
  682.1 7.7 fusion.163
  700.4 9.8 fusion.98
  711.6 19.3 %reduce-scatter.9.cloned.1.call-done = f32[512,256]{0,1:T(8,128)} async-done(((f32[2048,256]{0,1:T(8,128)}), f32[512,256]{0,1:T(8,128)}) %reduce-scatter.9.cloned.1.call-update) | async-done | bytes 524304 | tf_op jit(solution)/shard_map/reduce_scatter | solution.py:262
  745.5 285.0 %all-reduce.9.cloned.1.call-done = (f32[512,2048]{1,0:T(8,128)}, f32[512,2048]{1,0:T(8,128)}) async-done(((f32[512,2048]{1,0:T(8,128)}, f32[512,2048]{1,0:T(8,128)}), (f32[512,2048]{1,0:T(8,128)}, f32[512,2048]{1,0:T(8,128)})) %all-reduce.9.cloned.1.call-update) | async-done | bytes 8388624 | tf_op jit(solution)/shard_map/psum | solution.py:229
  1039.9 13.0 fusion.70
  1053.7 19.2 %fusion.66 = f32[2048,4096]{1,0:T(8,128)} fusion(bf16[512,2048]{1,0:T(8,128)(2,1)} %copy-done.37, bf16[512,2048]{1,0:T(8,128)(2,1)} %copy-done.36, f32[512,2048]{1,0:T(8,128)} %get-tuple-element.399, f32[2048]{0:T(1024)S(1)} %bitcast.254, f32[512]{0:T(512)S(1)} %copy-done.28), kind=kOutput, calls=%fused_computation.91 | convolution fusion | flops 8601468928 | bytes 41953280 | tf_op jit(solution)/shard_map/dot_general | solution.py:28
  1072.9 11.5 reduce-scatter.13.cloned.1.call-done
  1087.0 9.7 fusion.63
  1096.6 27.5 %reduce-scatter.19.cloned.1.call-done = f32[256,2]{1,0:T(8,128)} async-done(((f32[2048,2]{1,0:T(8,128)}), f32[256,2]{1,0:T(8,128)}) %reduce-scatter.19.cloned.1.call-update) | async-done | bytes 2064
  1125.8 63.4 %reduce-scatter.11.cloned.1.call-done = f32[256,768]{1,0:T(8,128)} async-done(((f32[2048,768]{1,0:T(8,128)}), f32[256,768]{1,0:T(8,128)}) %reduce-scatter.11.cloned.1.call-update) | async-done | bytes 786448 | tf_op jit(solution)/shard_map/reduce_scatter | solution.py:275
  1192.5 116.6 %reduce-scatter.17.cloned.1.call-done = f32[2048,256]{1,0:T(8,128)} async-done(((f32[2048,2048]{1,0:T(8,128)}), f32[2048,256]{1,0:T(8,128)}) %reduce-scatter.17.cloned.1.call-update) | async-done | bytes 2097168 | tf_op jit(solution)/shard_map/reduce_scatter | solution.py:278
  1315.7 202.6 %reduce-scatter.15.cloned.1.call-done = f32[256,4096]{1,0:T(8,128)} async-done(((f32[2048,4096]{1,0:T(8,128)}), f32[256,4096]{1,0:T(8,128)}) %reduce-scatter.15.cloned.1.call-update) | async-done | bytes 4194320 | tf_op jit(solution)/shard_map/reduce_scatter | solution.py:277
  1518.3 11.1 multiply_subtract_fusion
  (209 shorter events, 155.7 us)
Async XLA Ops:
  7.2 38.3 %all-gather.6.cloned.1.call-start = ((), (), s32[]{:S(2)}) async-start(), calls=%async_computation.6 | async-start | bytes 3538944 | tf_op jit(solution)/shard_map/all_gather | solution.py:190
  9.2 58.9 %all-gather.8.cloned.1.call-start = ((), (), s32[]{:S(2)}) async-start(), calls=%async_computation.7 | async-start | bytes 1310720 | tf_op jit(solution)/shard_map/all_gather | solution.py:210
  23.1 26.8 %copy-start.25 = (f32[512]{0:T(512)}, f32[512]{0:T(512)S(1)}, u32[]{:S(2)}) copy-start(f32[512]{0:T(512)S(1)} %add_rsqrt_fusion.1) | copy-start | bytes 6148
  24.1 31.2 %copy-start.14 = (f32[512,32]{0,1:T(8,128)}, f32[512,32]{0,1:T(8,128)S(1)}, u32[]{:S(2)}) copy-start(f32[512,32]{0,1:T(8,128)S(1)} %get-tuple-element.419) | copy-start | bytes 196612
  24.1 25.9 %copy-start.20 = (f32[1,2048]{1,0:T(1,128)}, f32[1,2048]{1,0:T(1,128)S(1)}, u32[]{:S(2)}) copy-start(f32[1,2048]{1,0:T(1,128)S(1)} %get-tuple-element.416) | copy-start | bytes 24580
  24.1 597.6 %copy-start.22 = (f32[1,2048]{1,0:T(1,128)}, f32[1,2048]{1,0:T(1,128)S(1)}, u32[]{:S(2)}) copy-start(f32[1,2048]{1,0:T(1,128)S(1)} %get-tuple-element.415) | copy-start | bytes 24580
  51.2 72.4 %all-gather.10.cloned.1.call-start = ((), (), s32[]{:S(2)}) async-start(), calls=%async_computation.8 | async-start | bytes 2359296 | tf_op jit(solution)/shard_map/all_gather | solution.py:191
  52.0 231.8 %all-reduce.5.cloned.1.call-start = ((), (), s32[]{:S(2)}) async-start(), calls=%async_computation.9 | async-start | bytes 8388608 | tf_op jit(solution)/shard_map/psum | solution.py:220
  128.7 246.5 %all-gather.12.cloned.1.call-start = ((), (), s32[]{:S(2)}) async-start(), calls=%async_computation.10 | async-start | bytes 18874368 | tf_op jit(solution)/shard_map/all_gather | solution.py:192
  132.5 151.3 %copy-start.3 = (bf16[1,512,2048]{2,1,0:T(8,128)(2,1)S(1)}, bf16[1,512,2048]{2,1,0:T(8,128)(2,1)}, u32[]{:S(2)}) copy-start(bf16[1,512,2048]{2,1,0:T(8,128)(2,1)} %param.24) | copy-start | bytes 6291460
  132.5 301.1 %all-gather.14.cloned.1.call-start = ((), (), s32[]{:S(2)}) async-start(), calls=%async_computation.11 | async-start | bytes 9437184 | tf_op jit(solution)/shard_map/all_gather | solution.py:193
  135.6 480.9 %all-reduce.7.cloned.1.call-start = ((), (), s32[]{:S(2)}) async-start(), calls=%async_computation.12 | async-start | bytes 8388608 | tf_op jit(solution)/shard_map/psum | solution.py:240
  288.6 333.1 %copy-start.27 = (f32[512]{0:T(512)}, f32[512]{0:T(512)S(1)}, u32[]{:S(2)}) copy-start(f32[512]{0:T(512)S(1)} %add_rsqrt_fusion) | copy-start | bytes 6148
  375.2 58.5 %copy-start.13 = (bf16[1,512,2048]{2,1,0:T(8,128)(2,1)S(1)}, bf16[1,512,2048]{2,1,0:T(8,128)(2,1)}, u32[]{:S(2)}) copy-start(bf16[1,512,2048]{2,1,0:T(8,128)(2,1)} %param.26) | copy-start | bytes 6291460
  461.4 269.6 %reduce-scatter.9.cloned.1.call-start = ((), (), s32[]{:S(2)}) async-start(), calls=%async_computation.13 | async-start | bytes 2621440 | tf_op jit(solution)/shard_map/reduce_scatter | solution.py:262
  700.3 330.1 %all-reduce.9.cloned.1.call-start = ((), (), s32[]{:S(2)}) async-start(), calls=%async_computation.19 | async-start | bytes 16777216 | tf_op jit(solution)/shard_map/psum | solution.py:229
  738.7 345.6 %reduce-scatter.13.cloned.1.call-start = ((), (), s32[]{:S(2)}) async-start(), calls=%async_computation.15 | async-start | bytes 4718592 | tf_op jit(solution)/shard_map/reduce_scatter | solution.py:276
  745.4 285.1 %copy-start.4 = (bf16[1,512,2048]{2,1,0:T(8,128)(2,1)S(1)}, bf16[1,512,2048]{2,1,0:T(8,128)(2,1)}, u32[]{:S(2)}) copy-start(bf16[1,512,2048]{2,1,0:T(8,128)(2,1)} %param.24) | copy-start | bytes 6291460
  745.4 285.1 %copy-start.21 = (f32[1,2048]{1,0:T(1,128)S(1)}, f32[1,2048]{1,0:T(1,128)}, u32[]{:S(2)}) copy-start(f32[1,2048]{1,0:T(1,128)} %copy-done.20) | copy-start | bytes 24580
  745.4 285.1 %copy-start.26 = (f32[512]{0:T(512)S(1)}, f32[512]{0:T(512)}, u32[]{:S(2)}) copy-start(f32[512]{0:T(512)} %copy-done.25) | copy-start | bytes 6148
  745.4 288.3 %copy-start.24 = (f32[2048]{0:T(1024)S(1)}, f32[2048]{0:T(1024)}, u32[]{:S(2)}) copy-start(f32[2048]{0:T(1024)} %get-tuple-element.325) | copy-start | bytes 24580
  745.4 378.8 %reduce-scatter.19.cloned.1.call-start = ((), (), s32[]{:S(2)}) async-start(), calls=%async_computation.18 | async-start | bytes 1179648
  1035.1 154.0 %reduce-scatter.11.cloned.1.call-start = ((), (), s32[]{:S(2)}) async-start(), calls=%async_computation.14 | async-start | bytes 7077888 | tf_op jit(solution)/shard_map/reduce_scatter | solution.py:275
  1039.9 269.3 %reduce-scatter.17.cloned.1.call-start = ((), (), s32[]{:S(2)}) async-start(), calls=%async_computation.17 | async-start | bytes 18874368 | tf_op jit(solution)/shard_map/reduce_scatter | solution.py:278
  1053.0 465.3 %reduce-scatter.15.cloned.1.call-start = ((), (), s32[]{:S(2)}) async-start(), calls=%async_computation.16 | async-start | bytes 37748736 | tf_op jit(solution)/shard_map/reduce_scatter | solution.py:277
  1072.8 11.5 copy-start.11
  1072.8 11.5 copy-start.19
  1086.9 38.2 %copy-start.32 = (f32[2,256]{1,0:T(2,128)S(1)}, f32[2,256]{1,0:T(2,128)}, u32[]{:S(2)}) copy-start(f32[2,256]{1,0:T(2,128)} %param.39) | copy-start | bytes 6148
  1086.9 38.2 %copy-start.33 = (f32[2,256]{1,0:T(2,128)S(1)}, f32[2,256]{1,0:T(2,128)}, u32[]{:S(2)}) copy-start(f32[2,256]{1,0:T(2,128)} %param.41) | copy-start | bytes 6148
  1087.0 38.2 %copy-start.34 = (f32[2,256]{1,0:T(2,128)S(1)}, f32[2,256]{1,0:T(2,128)}, u32[]{:S(2)}) copy-start(f32[2,256]{1,0:T(2,128)} %param.40) | copy-start | bytes 6148
  1087.0 102.2 %copy-start.9 = (f32[256,768]{1,0:T(8,128)S(1)}, f32[256,768]{1,0:T(8,128)}, u32[]{:S(2)}) copy-start(f32[256,768]{1,0:T(8,128)} %param.27) | copy-start | bytes 2359300
  1096.6 212.5 %copy-start.6 = (f32[2048,256]{1,0:T(8,128)S(1)}, f32[2048,256]{1,0:T(8,128)}, u32[]{:S(2)}) copy-start(f32[2048,256]{1,0:T(8,128)} %param.36) | copy-start | bytes 6291460
  (23 other events, 96.5 us)
Sparse Core Ops, SparseCore 0:
  10.5 35.0 all-gather.5
  51.3 16.7 all-gather.7
  70.6 28.1 all-gather.9
  128.8 154.9 all-reduce.4
  286.3 88.8 all-gather.11
  377.6 55.9 all-gather.13
  461.5 154.9 all-reduce.6
  700.5 30.4 reduce-scatter.8
  738.8 291.5 all-reduce.8
  1034.0 50.3 reduce-scatter.12
  1088.1 36.0 reduce-scatter.18
  1127.4 61.7 reduce-scatter.10
  1193.1 115.9 reduce-scatter.16
  1313.0 205.2 reduce-scatter.14
where the time goes:
time: 1540 us
  waiting for transfers between devices  1190 us (77%)
  matrix products  208 us (14%)
  other arithmetic  84.4 us (5%)
  local copies, waits for them, and re-layouts  25.2 us (2%)
    psum x1, waiting for transfers between devices, local(): lax.psum(jnp.dot(activated, full_down, preferred_element_type=jnp.float32...  285 us
    reduce_scatter x1, waiting for transfers between devices, local(): lax.psum_scatter(grad_gate_up, ('dp', 'ctx'), scatter_dimension=0, tiled=...  203 us
    psum x1, waiting for transfers between devices, local(): d_normed_two = lax.psum(contract(d_gate_up, full_gate_up, 1, 1), 'tensor')  155 us
    psum x1, waiting for transfers between devices, local(): lax.psum(jnp.dot(attn_in, full_out, preferred_element_type=jnp.float32),...  148 us
    reduce_scatter x1, waiting for transfers between devices, local(): lax.psum_scatter(grad_down, ('dp', 'ctx'), scatter_dimension=1, tiled=True)  117 us
    all_gather x1, waiting for transfers between devices, local(): lax.all_gather(w_gate_up.astype(jnp.bfloat16), ('dp', 'ctx'), axis=0, til...  86.6 us
    dot_general x8, matrix products, contract(): lax.dot_general(left, right, (((left_dim,), (right_dim,)), ((), ())), pre...  76.7 us
    reduce_scatter x1, waiting for transfers between devices, local(): lax.psum_scatter(grad_qkv, ('dp', 'ctx'), scatter_dimension=0, tiled=True)  63.4 us
  transfers between devices with their start and end apart: 14, of which 13 were waited for; matrix products, arithmetic and copies ran while one was open for 11% of the time, Pallas kernels for 0%

commit v1 on v0

v1 whole, which is shorter than its diff:
```python
import functools
import math

import jax
import jax.numpy as jnp
from jax import lax
from jax.experimental import pallas as pl
from jax.experimental.pallas import tpu as pltpu
from jax.sharding import PartitionSpec as P

HQ = 32
KV = 8
HD = 64
FF = 8192
STEP = 10
RUN = 256


NORM_EPS = 1e-05
ROPE_THETA = 500000.0
SCORE_SCALE = 0.125
LEARN_RATE = 0.01
OUT_RATE = 0.05
GAIN_RATE = 0.25
BETA_ONE = 0.9
BETA_TWO = 0.95
ADAM_EPS = 1e-08
WEIGHT_DECAY = 0.1

F32 = jnp.float32
LOW = jnp.bfloat16


def contract(left, right, left_dim, right_dim):
    return lax.dot_general(
        left, right, (((left_dim,), (right_dim,)), ((), ())), preferred_element_type=F32
    )


def rotary_tables(places):
    half = HD // 2
    freqs = ROPE_THETA ** (-(jnp.arange(half, dtype=F32) * 2.0 / HD))
    angles = freqs[:, None] * places.astype(F32)[None, :]
    return jnp.cos(angles), jnp.sin(angles)


def rotate(vectors, cosine, sine):
    half = HD // 2
    first = vectors[..., :half, :]
    second = vectors[..., half:, :]
    return jnp.concatenate(
        [first * cosine - second * sine, second * cosine + first * sine], axis=-2
    )


def normalize(values):
    factor = lax.rsqrt(jnp.mean(values * values, axis=-1, keepdims=True) + NORM_EPS)
    return (values * factor, factor)


def norm_back(grad_hat, x_hat, factor):
    return factor * (grad_hat - x_hat * jnp.mean(grad_hat * x_hat, axis=-1, keepdims=True))


def adamw_step(weight, first, second, gradient, step_rate, decay_rate):
    first_new = BETA_ONE * first + (1.0 - BETA_ONE) * gradient
    second_new = BETA_TWO * second + (1.0 - BETA_TWO) * gradient * gradient
    first_hat = first_new / (1.0 - BETA_ONE**STEP)
    second_hat = second_new / (1.0 - BETA_TWO**STEP)
    weight_new = weight - step_rate * (
        first_hat / (jnp.sqrt(second_hat) + ADAM_EPS) + decay_rate * weight
    )
    return (first_new, second_new, weight_new)


def shift_pairs(count, step):
    return [(i, (i + step) % count) for i in range(count)]


def flip_pairs(count, mask):
    return [(i, i ^ mask) for i in range(count)]


def cut(parts, index, rows):
    return lax.dynamic_slice_in_dim(parts, index * rows, rows)


def scatter_begin(parts, axis):
    count = lax.axis_size(axis)
    blocks = parts
    if not isinstance(parts, (list, tuple)):
        rows = parts.shape[0] // count
        blocks = [parts[step * rows : (step + 1) * rows] for step in range(count)]
    own = blocks[0]
    if count == 4:
        through = lax.ppermute(blocks[3].astype(LOW), axis, flip_pairs(count, 1))
        return [own, blocks[1].astype(LOW), through, blocks[2]]
    return [own] + [
        lax.ppermute(blocks[step].astype(LOW), axis, shift_pairs(count, step))
        for step in range(1, count)
    ]


def scatter_middle(pieces, axis):
    count = lax.axis_size(axis)
    if count == 4:
        own, near, through, far = pieces
        near, through = lax.optimization_barrier((near, through))
        joined = (far.astype(F32) + through.astype(F32)).astype(LOW)
        return [
            own,
            lax.ppermute(near, axis, flip_pairs(count, 1)),
            lax.ppermute(joined, axis, flip_pairs(count, 2)),
        ]
    return pieces


def scatter_end(pieces):
    total = pieces[0].astype(F32)
    for piece in pieces[1:]:
        total = total + piece.astype(F32)
    return total


def sum_scatter(parts, axis):
    return scatter_end(scatter_middle(scatter_begin(parts, axis), axis))


def gains_scatter(parts, axis):
    count = lax.axis_size(axis)
    here = lax.axis_index(axis)
    rows = parts.shape[0] // count
    total = cut(parts, here, rows)
    for step in range(1, count):
        piece = cut(parts, lax.rem(here + step, count), rows)
        total = total + lax.ppermute(piece, axis, shift_pairs(count, step))
    return total


def sum_everywhere(values, axis):
    count = lax.axis_size(axis)
    total = values
    for step in range(1, count):
        total = total + lax.ppermute(values, axis, shift_pairs(count, step))
    return total


def blocks_from_here(count, here, rows, values, axis=0):
    cuts = []
    for step in range(count):
        index = here ^ step if count == 4 else lax.rem(here + step, count)
        cuts.append(lax.dynamic_slice_in_dim(values, index * rows, rows, axis))
    return jnp.concatenate(cuts, axis=axis)


def axis_peers(axis):
    count, here = lax.axis_size(axis), lax.axis_index(axis)
    return jnp.stack(
        [here ^ step if count == 4 else lax.rem(here + step, count) for step in range(count)]
    ).astype(jnp.int32)


def gather_blocks(rows, axis):
    count = lax.axis_size(axis)
    if count == 4:
        near = lax.ppermute(rows, axis, flip_pairs(count, 1))
        far = lax.ppermute(rows, axis, flip_pairs(count, 2))
        near, far = lax.optimization_barrier((near, far))
        last = lax.ppermute(far, axis, flip_pairs(count, 1))
        return [rows, near, far, last]
    return [rows] + [
        lax.ppermute(rows, axis, shift_pairs(count, count - step)) for step in range(1, count)
    ]


def place_blocks(blocks, axis):
    count = lax.axis_size(axis)
    here = lax.axis_index(axis)
    size = blocks[0].shape[0]
    whole_rows = jnp.zeros((count * size,) + blocks[0].shape[1:], blocks[0].dtype)
    for step, block in enumerate(blocks):
        index = here ^ step if count == 4 else lax.rem(here + step, count)
        whole_rows = lax.dynamic_update_slice_in_dim(whole_rows, block, index * size, 0)
    return whole_rows


def spread(rows, axis):
    return place_blocks(gather_blocks(rows, axis), axis)


def block_place(order_ref, rank, per_device):
    run = order_ref[rank]
    return run // per_device, pl.multiple_of((run % per_device) * RUN, RUN)


def dot_nn(left, right):
    return jnp.dot(left, right, preferred_element_type=F32)


def dot_nt(left, right):
    return lax.dot_general(left, right, (((1,), (1,)), ((), ())), preferred_element_type=F32)


def causal_mask(columns):
    keys = lax.broadcasted_iota(jnp.int32, (RUN, columns), 0)
    queries = lax.broadcasted_iota(jnp.int32, (RUN, columns), 1) & (RUN - 1)
    return keys <= queries


def take_blocks(peer_ref, piece_refs, kvn_ref, kvt_ref):
    for block, piece_ref in enumerate(piece_refs):
        kvt_ref[peer_ref[block]] = piece_ref[0]
        kvn_ref[peer_ref[block]] = piece_ref[0].T


def head_columns(head):
    return slice(head * RUN, (head + 1) * RUN)


def forward_kernel(devices, per_device, ratio, order_ref, rank_ref, peer_ref, *refs):
    piece_refs = refs[:devices]
    q_ref, mix_ref, low_ref, lse_ref, q_pad, high, total, summed, kvn_ref, kvt_ref = refs[devices:]
    rank = rank_ref[pl.program_id(1)]

    @pl.when(pl.program_id(1) == 0)
    def _():
        take_blocks(peer_ref, piece_refs, kvn_ref, kvt_ref)

    for head in range(ratio):
        q_pad[:HD, head_columns(head)] = q_ref[0, head]
    q_pad[HD:] = jnp.zeros((HD, ratio * RUN), LOW)

    def visit(step, first):
        device, offset = block_place(order_ref, step, per_device)
        keys = kvn_ref[device, pl.ds(offset, RUN), :]
        values = kvt_ref[device, HD:, pl.ds(offset, RUN)]
        scores = dot_nn(keys, q_pad[...])
        if first:
            scores = jnp.where(causal_mask(ratio * RUN), scores, -1e30)
        top = jnp.max(scores, axis=0, keepdims=True)
        if not first:
            old = high[...]
            top = jnp.maximum(old, top)
            scale = jnp.exp(old - top)
        probs = jnp.exp(scores - top)
        row_sum = jnp.sum(probs, axis=0, keepdims=True)
        product = dot_nn(values, probs.astype(LOW))
        high[...] = top
        if first:
            total[...] = row_sum
            summed[...] = product
        else:
            total[...] = total[...] * scale + row_sum
            summed[...] = summed[...] * scale + product

    visit(rank, True)

    @pl.loop(0, rank)
    def _(step):
        visit(step, False)

    mixed = summed[...] / total[...]
    log_total = high[...] + jnp.log(total[...])
    for head in range(ratio):
        mix_ref[0, head] = mixed[:, head_columns(head)]
        low_ref[0, head] = mixed[:, head_columns(head)].astype(LOW)
        lse_ref[0, head] = log_total[:, head_columns(head)]


def backward_kernel(devices, per_device, ratio, earlier, order_ref, rank_ref, peer_ref, *refs):
    piece_refs, refs = refs[:devices], refs[devices:]
    earlier_refs, refs = refs[:earlier], refs[earlier:]
    q_ref, d_ref, mix_ref, lse_ref, cos_ref, sin_ref, dq_ref = refs[:7]
    dkv_refs = refs[7:-7]
    pads, row_dot, log_total, dq_sum, dkv_sum, kvn_ref, kvt_ref = refs[-7:]
    place = pl.program_id(0)
    rank = rank_ref[place]
    columns = ratio * RUN

    @pl.when(place == 0)
    def _():
        dkv_sum[...] = jnp.zeros_like(dkv_sum)
        take_blocks(peer_ref, piece_refs, kvn_ref, kvt_ref)

    pads[HD:, :columns] = jnp.zeros((HD, columns), LOW)
    pads[:HD, columns:] = jnp.zeros((HD, columns), LOW)
    for head in range(ratio):
        here = head_columns(head)
        pads[:HD, here] = q_ref[0, head]
        pads[HD:, head_columns(ratio + head)] = d_ref[0, head]
        row_dot[:, here] = jnp.sum(
            d_ref[0, head].astype(F32) * mix_ref[0, head], axis=0, keepdims=True
        )
        log_total[:, here] = lse_ref[0, head]

    def visit(step, first):
        device, offset = block_place(order_ref, step, per_device)
        rows = kvn_ref[device, pl.ds(offset, RUN), :]
        keys = kvt_ref[device, :HD, pl.ds(offset, RUN)]
        probs = jnp.exp(dot_nn(rows, pads[:, :columns]) - log_total[...])
        if first:
            probs = jnp.where(causal_mask(columns), probs, 0.0)
        d_probs = dot_nn(rows, pads[:, columns:])
        d_scores = (probs * (d_probs - row_dot[...])).astype(LOW)
        product = dot_nn(keys, d_scores)
        if first:
            dq_sum[...] = product
        else:
            dq_sum[...] += product
        dkv_sum[device, pl.ds(offset, RUN), :] += dot_nt(
            jnp.concatenate([d_scores, probs.astype(LOW)], axis=1), pads[...]
        )

    visit(rank, True)

    @pl.loop(0, rank)
    def _(step):
        visit(step, False)

    half = HD // 2
    for head in range(ratio):
        first = dq_sum[:half, head_columns(head)] * SCORE_SCALE
        second = dq_sum[half:, head_columns(head)] * SCORE_SCALE
        dq_ref[0, head, :half] = (first * cos_ref[...] + second * sin_ref[...]).astype(LOW)
        dq_ref[0, head, half:] = (second * cos_ref[...] - first * sin_ref[...]).astype(LOW)

    @pl.when(place == pl.num_programs(0) - 1)
    def _():
        for block, dkv_ref in enumerate(dkv_refs):
            start = 0
            if earlier:
                start = earlier_refs[block].shape[0]
                dkv_ref[:start] = earlier_refs[block][...]
            dkv_ref[start:] = dkv_sum[peer_ref[block]].T.astype(LOW)


VMEM_LIMIT = 48 * 1024 * 1024
SMALL_COST = pl.CostEstimate(flops=1000, bytes_accessed=1000, transcendentals=0)


def attend_forward(order, ranks, peers, queries, kv_blocks):
    groups, ratio, head_size, tokens = queries.shape
    devices = len(kv_blocks)
    width, per_tokens = kv_blocks[0].shape[1:]
    q_spec = pl.BlockSpec((1, ratio, HD, RUN), lambda g, i, *s: (g, 0, 0, i))
    blocks = groups * (tokens // RUN) * devices * (per_tokens // RUN) * ratio
    return pl.pallas_call(
        functools.partial(forward_kernel, devices, per_tokens // RUN, ratio),
        grid_spec=pltpu.PrefetchScalarGridSpec(
            num_scalar_prefetch=3,
            grid=(groups, tokens // RUN),
            in_specs=[pl.BlockSpec((1, width, per_tokens), lambda g, i, *s: (g, 0, 0))] * devices
            + [q_spec],
            out_specs=[
                q_spec,
                q_spec,
                pl.BlockSpec((1, ratio, 1, RUN), lambda g, i, *s: (g, 0, 0, i)),
            ],
            scratch_shapes=[
                pltpu.VMEM((2 * HD, ratio * RUN), LOW),
                pltpu.VMEM((1, ratio * RUN), F32),
                pltpu.VMEM((1, ratio * RUN), F32),
                pltpu.VMEM((HD, ratio * RUN), F32),
                pltpu.VMEM((devices, per_tokens, width), LOW),
                pltpu.VMEM((devices, width, per_tokens), LOW),
            ],
        ),
        out_shape=[
            jax.ShapeDtypeStruct(queries.shape, F32),
            jax.ShapeDtypeStruct(queries.shape, LOW),
            jax.ShapeDtypeStruct((groups, ratio, 1, tokens), F32),
        ],
        compiler_params=pltpu.CompilerParams(
            dimension_semantics=("arbitrary", "arbitrary"), vmem_limit_bytes=VMEM_LIMIT
        ),
        cost_estimate=pl.CostEstimate(
            flops=blocks * 64 * RUN * RUN * HD,
            bytes_accessed=8 * 1024 * 1024,
            transcendentals=blocks * RUN * RUN,
        ),
        name="attend_forward",
    )(order, ranks, peers, *kv_blocks, queries)


def attend_backward(
    group, order, ranks, peers, kv_blocks, earlier, queries, d_mixed, mixed, log_total, cosine,
    sine, *deps,
):
    groups, ratio, head_size, tokens = queries.shape
    devices = len(kv_blocks)
    width, per_tokens = kv_blocks[0].shape[1:]
    q_spec = pl.BlockSpec((1, ratio, HD, RUN), lambda i, *s: (group, 0, 0, i))
    table = pl.BlockSpec((HD // 2, RUN), lambda i, *s: (0, i))
    blocks = (tokens // RUN) * devices * (per_tokens // RUN) * ratio
    grown = width + (earlier[0].shape[0] if earlier else 0)
    inputs = [*kv_blocks, *earlier, queries, d_mixed, mixed, log_total, cosine, sine]
    return pl.pallas_call(
        with_deps(
            functools.partial(backward_kernel, devices, per_tokens // RUN, ratio, len(earlier)),
            len(inputs),
            len(deps),
            3,
        ),
        grid_spec=pltpu.PrefetchScalarGridSpec(
            num_scalar_prefetch=3,
            grid=(tokens // RUN,),
            in_specs=[pl.BlockSpec((1, width, per_tokens), lambda i, *s: (group, 0, 0))] * devices
            + [pl.BlockSpec(each.shape, lambda i, *s: (0, 0)) for each in earlier]
            + [q_spec] * 3
            + [pl.BlockSpec((1, ratio, 1, RUN), lambda i, *s: (group, 0, 0, i)), table, table]
            + [pl.BlockSpec(memory_space=pl.ANY)] * len(deps),
            out_specs=[pl.BlockSpec((1, ratio, HD, RUN), lambda i, *s: (0, 0, 0, i))]
            + [pl.BlockSpec((grown, per_tokens), lambda i, *s: (0, 0))] * devices,
            scratch_shapes=[
                pltpu.VMEM((2 * HD, 2 * ratio * RUN), LOW),
                pltpu.VMEM((1, ratio * RUN), F32),
                pltpu.VMEM((1, ratio * RUN), F32),
                pltpu.VMEM((HD, ratio * RUN), F32),
                pltpu.VMEM((devices, per_tokens, width), F32),
                pltpu.VMEM((devices, per_tokens, width), LOW),
                pltpu.VMEM((devices, width, per_tokens), LOW),
            ],
        ),
        out_shape=[jax.ShapeDtypeStruct((1,) + queries.shape[1:], LOW)]
        + [jax.ShapeDtypeStruct((grown, per_tokens), LOW)] * devices,
        compiler_params=pltpu.CompilerParams(
            dimension_semantics=("arbitrary",), vmem_limit_bytes=VMEM_LIMIT
        ),
        cost_estimate=pl.CostEstimate(
            flops=blocks * 128 * RUN * RUN * HD,
            bytes_accessed=8 * 1024 * 1024,
            transcendentals=blocks * RUN * RUN,
        ),
        name="attend_backward",
    )(order, ranks, peers, *inputs, *deps)


TILE = 256


def whole(shape):
    return pl.BlockSpec(shape, lambda j: (0,) * len(shape), pipeline_mode=pl.Buffered(1))


def with_deps(kernel, inputs, deps, scalars=0):
    first = scalars + inputs

    def run(*refs):
        kernel(*refs[:first], *refs[first + deps :])

    return run


def tile_call(kernel, name, tiles, in_specs, out_specs, out_shape, flops, scratch=(), deps=0):
    size = sum(math.prod(each.shape) * each.dtype.itemsize for each in out_shape)
    return pl.pallas_call(
        with_deps(kernel, len(in_specs), deps),
        grid=(tiles,),
        in_specs=list(in_specs) + [pl.BlockSpec(memory_space=pl.ANY)] * deps,
        out_specs=out_specs,
        out_shape=out_shape,
        scratch_shapes=scratch,
        compiler_params=pltpu.CompilerParams(
            dimension_semantics=("arbitrary",), vmem_limit_bytes=VMEM_LIMIT
        ),
        cost_estimate=pl.CostEstimate(
            flops=flops * 3 // 2, bytes_accessed=2 * size, transcendentals=0
        ),
        name=name,
    )


def held_until_kernel(values_ref, *refs):
    mark_ref = refs[-1]
    mark_ref[...] = jnp.zeros_like(mark_ref)


def held_until(values, *deps):
    hidden = pl.BlockSpec(memory_space=pl.ANY)
    return pl.pallas_call(
        held_until_kernel,
        in_specs=[hidden] * (1 + len(deps)),
        out_specs=[hidden, pl.BlockSpec(memory_space=pltpu.VMEM)],
        out_shape=[
            jax.ShapeDtypeStruct(values.shape, values.dtype),
            jax.ShapeDtypeStruct((8, 128), F32),
        ],
        input_output_aliases={0: 0},
        name="held_until",
    )(values, *deps)[0]


def store_blocks(out_refs, values):
    rows = out_refs[0].shape[0]
    for block, out_ref in enumerate(out_refs):
        out_ref[...] = values[block * rows : (block + 1) * rows].astype(out_ref.dtype)


def block_shapes(blocks, rows, width):
    kept = (0, 2) if blocks == 4 else (0,)
    return [
        jax.ShapeDtypeStruct((rows, width), F32 if block in kept else LOW)
        for block in range(blocks)
    ]


def ffn_both_kernel(blocks, tiles, *refs):
    x_refs = refs[:blocks]
    g_ref, gate_ref, up_ref, down_ref, gate_rows_ref, up_rows_ref = refs[blocks : blocks + 6]
    active_ref, d_gate_ref, d_up_ref = refs[blocks + 6 : blocks + 9]
    out_refs = refs[blocks + 9 : -3]
    x_all, d_gate_all, d_up_all = refs[-3:]
    step = pl.program_id(0)
    rows = x_refs[0].shape[0]

    @pl.when(step == 0)
    def _():
        for block in range(blocks):
            x_all[block * rows : (block + 1) * rows] = x_refs[block][...]

    @pl.when(step < tiles)
    def _():
        gate = dot_nn(x_all[...], gate_ref[...])
        up = dot_nn(x_all[...], up_ref[...])
        d_act = dot_nn(g_ref[...], down_ref[...])
        sigmoid = 1.0 / (1.0 + jnp.exp(-gate))
        silu = gate * sigmoid
        d_gate = (d_act * up * sigmoid * (1.0 + gate * (1.0 - sigmoid))).astype(LOW)
        d_up = (d_act * silu).astype(LOW)
        columns = pl.ds(pl.multiple_of(step * TILE, TILE), TILE)
        active_ref[...] = (silu * up).astype(LOW)
        d_gate_ref[...] = d_gate
        d_up_ref[...] = d_up
        d_gate_all[:, columns] = d_gate
        d_up_all[:, columns] = d_up

    @pl.when(step >= tiles)
    def _():
        store_blocks(
            out_refs,
            dot_nt(d_gate_all[...], gate_rows_ref[...]) + dot_nt(d_up_all[...], up_rows_ref[...]),
        )


def ffn_both(x_blocks, g_rows, weights):
    blocks = len(x_blocks)
    rows, width = x_blocks[0].shape
    tokens = g_rows.shape[0]
    units = weights.shape[1] // 3
    tiles = units // TILE

    def columns(part):
        return pl.BlockSpec(
            (width, TILE), lambda j: (0, jnp.minimum(j, tiles - 1) + part * tiles)
        )

    def weight_rows(part):
        return pl.BlockSpec((TILE, units), lambda j: (jnp.maximum(j - tiles, 0), part))

    outs = tile_call(
        functools.partial(ffn_both_kernel, blocks, tiles),
        "ffn_both",
        tiles + width // TILE,
        [whole((rows, width))] * blocks
        + [whole((tokens, width)), columns(0), columns(1), columns(2)]
        + [weight_rows(0), weight_rows(1)],
        [pl.BlockSpec((tokens, TILE), lambda j: (0, jnp.minimum(j, tiles - 1)))] * 3
        + [pl.BlockSpec((rows, TILE), lambda j: (0, jnp.maximum(j - tiles, 0)))] * blocks,
        [jax.ShapeDtypeStruct((tokens, units), LOW)] * 3 + block_shapes(blocks, rows, width),
        10 * tokens * width * units,
        [pltpu.VMEM((tokens, width), LOW)] + [pltpu.VMEM((tokens, units), LOW)] * 2,
    )(*x_blocks, g_rows, *([weights] * 5))
    return outs[0], outs[1], outs[2], outs[3:]


def ffn_out_kernel(active_ref, down_ref, *out_refs):
    store_blocks(out_refs, dot_nt(active_ref[...], down_ref[...]))


def ffn_out(blocks, active, weights, *deps):
    tokens, units = active.shape
    width = weights.shape[0]
    rows = tokens // blocks
    return tile_call(
        ffn_out_kernel,
        "ffn_out",
        width // TILE,
        [whole((tokens, units)), pl.BlockSpec((TILE, units), lambda j: (j, 2))],
        [pl.BlockSpec((rows, TILE), lambda j: (0, j))] * blocks,
        block_shapes(blocks, rows, width),
        2 * tokens * width * units,
        deps=len(deps),
    )(active, weights, *deps)


def ffn_grads_kernel(blocks, *refs):
    x_refs = refs[:blocks]
    g_ref, active_ref, d_gate_ref, d_up_ref, grads_ref, mark_ref = refs[blocks:]
    mark_ref[...] = jnp.zeros_like(mark_ref)
    units = active_ref.shape[1]
    x_turned = jnp.concatenate([x_ref[...] for x_ref in x_refs], axis=0).T
    grads_ref[:, :units] = dot_nn(x_turned, d_gate_ref[...]).astype(LOW)
    grads_ref[:, units : 2 * units] = dot_nn(x_turned, d_up_ref[...]).astype(LOW)
    grads_ref[:, 2 * units :] = dot_nn(g_ref[...].T, active_ref[...]).astype(LOW)


def ffn_grads(x_blocks, g_rows, active, d_gate, d_up, *deps):
    blocks = len(x_blocks)
    rows, width = x_blocks[0].shape
    tokens, units = active.shape
    return tile_call(
        functools.partial(ffn_grads_kernel, blocks),
        "ffn_grads",
        width // TILE,
        [pl.BlockSpec((rows, TILE), lambda j: (0, j))] * blocks
        + [pl.BlockSpec((tokens, TILE), lambda j: (0, j))]
        + [whole((tokens, units))] * 3,
        [pl.BlockSpec((TILE, 3 * units), lambda j: (j, 0)), whole((8, 128))],
        [
            jax.ShapeDtypeStruct((width, 3 * units), LOW),
            jax.ShapeDtypeStruct((8, 128), F32),
        ],
        6 * tokens * width * units,
        deps=len(deps),
    )(*x_blocks, g_rows, active, d_gate, d_up, *deps)


def row_grads_kernel(blocks, turned, adds, order_ref, *refs):
    left_refs = refs[:blocks]
    right_ref = refs[blocks]
    left = jnp.concatenate([left_ref[...] for left_ref in left_refs], axis=0).T
    dot = dot_nt if turned else dot_nn
    grad = dot(left, right_ref[...])
    if adds:
        got_ref, kept_ref, sent_ref = refs[blocks + 1 :]
        grad = grad + got_ref[0].astype(F32)

        @pl.when(pl.program_id(0) < 2)
        def _():
            kept_ref[0] = grad

        @pl.when(pl.program_id(0) >= 2)
        def _():
            sent_ref[0] = grad.astype(LOW)

        return
    refs[blocks + 1][0] = grad.astype(LOW)


def row_grads(left_blocks, right, turned, order, got, name, *deps):
    blocks = len(left_blocks)
    rows = left_blocks[0].shape[0]
    columns = right.shape[0] if turned else right.shape[1]
    size = left_blocks[0].shape[1] // 8
    block = pl.BlockSpec((1, size, columns), lambda j, o: (j, 0, 0))
    in_specs = [pl.BlockSpec((rows, size), lambda j, o: (0, o[j]))] * blocks + [
        pl.BlockSpec(right.shape, lambda j, o: (0, 0))
    ]
    inputs = [*left_blocks, right]
    if got is None:
        out_specs = [block]
        out_shape = [jax.ShapeDtypeStruct((4, size, columns), LOW)]
    else:
        in_specs.append(block)
        inputs.append(got)
        out_specs = [
            pl.BlockSpec((1, size, columns), lambda j, o: (jnp.minimum(j, 1), 0, 0)),
            pl.BlockSpec((1, size, columns), lambda j, o: (jnp.maximum(j, 2) - 2, 0, 0)),
        ]
        out_shape = [
            jax.ShapeDtypeStruct((2, size, columns), F32),
            jax.ShapeDtypeStruct((2, size, columns), LOW),
        ]
    kernel = functools.partial(row_grads_kernel, blocks, turned, got is not None)
    kernel = with_deps(kernel, len(inputs), len(deps), 1)
    in_specs += [pl.BlockSpec(memory_space=pl.ANY)] * len(deps)
    return pl.pallas_call(
        kernel,
        grid_spec=pltpu.PrefetchScalarGridSpec(
            num_scalar_prefetch=1, grid=(4,), in_specs=in_specs, out_specs=out_specs
        ),
        out_shape=out_shape,
        compiler_params=pltpu.CompilerParams(
            dimension_semantics=("arbitrary",), vmem_limit_bytes=VMEM_LIMIT
        ),
        cost_estimate=SMALL_COST,
        name=name,
    )(order, *inputs, *deps)


def project_back_kernel(blocks, groups, terms, peer_ref, *refs):
    q_refs, refs = refs[:groups], refs[groups:]
    term_refs, refs = refs[:terms], refs[terms:]
    cos_ref, sin_ref, w_ref = refs[:3]
    out_refs = refs[3 : 3 + blocks]
    d_projected_ref, turned, placed = refs[3 + blocks :]
    heads = q_refs[0].shape[0]
    rows = out_refs[0].shape[0]
    half = HD // 2

    @pl.when(pl.program_id(0) == 0)
    def _():
        for group in range(groups):
            d_projected_ref[group * heads : (group + 1) * heads] = q_refs[group][...]
            part = pl.ds(group * 2 * HD, 2 * HD)
            total = term_refs[0][part, :].astype(F32)
            for term_ref in term_refs[1:]:
                total = total + term_ref[part, :].astype(F32)
            first, second = total[:half], total[half:HD]
            key = groups * heads + group * HD
            d_projected_ref[key : key + half] = (
                first * cos_ref[...] + second * sin_ref[...]
            ).astype(LOW)
            d_projected_ref[key + half : key + HD] = (
                second * cos_ref[...] - first * sin_ref[...]
            ).astype(LOW)
            d_projected_ref[key + groups * HD : key + (groups + 1) * HD] = total[HD:].astype(LOW)
        turned[...] = d_projected_ref[...].T
        for block in range(blocks):
            start = pl.multiple_of(peer_ref[block] * rows, rows)
            placed[block * rows : (block + 1) * rows] = turned[pl.ds(start, rows)]

    store_blocks(out_refs, dot_nt(placed[...], w_ref[...]))


def project_back(peers, d_query, kv_terms, cosine, sine, weights, *deps):
    blocks, groups, terms = peers.shape[0], len(d_query), len(kv_terms)
    heads, tokens = d_query[0].shape
    columns = groups * (heads + 2 * HD)
    width = weights.shape[0]
    rows = tokens // blocks
    inputs = [*d_query, *kv_terms, cosine, sine]
    outs = pl.pallas_call(
        with_deps(
            functools.partial(project_back_kernel, blocks, groups, terms),
            len(inputs) + 1,
            len(deps),
            1,
        ),
        grid_spec=pltpu.PrefetchScalarGridSpec(
            num_scalar_prefetch=1,
            grid=(width // TILE,),
            in_specs=[pl.BlockSpec(each.shape, lambda j, o: (0, 0)) for each in inputs]
            + [pl.BlockSpec((TILE, columns), lambda j, o: (j, 0))]
            + [pl.BlockSpec(memory_space=pl.ANY)] * len(deps),
            out_specs=[pl.BlockSpec((rows, TILE), lambda j, o: (0, j))] * blocks
            + [pl.BlockSpec((columns, tokens), lambda j, o: (0, 0))],
            scratch_shapes=[
                pltpu.VMEM((tokens, columns), LOW),
                pltpu.VMEM((tokens, columns), LOW),
            ],
        ),
        out_shape=block_shapes(blocks, rows, width)
        + [jax.ShapeDtypeStruct((columns, tokens), LOW)],
        compiler_params=pltpu.CompilerParams(
            dimension_semantics=("arbitrary",), vmem_limit_bytes=VMEM_LIMIT
        ),
        cost_estimate=SMALL_COST,
        name="project_back",
    )(peers, *inputs, weights, *deps)
    return outs[:blocks], outs[blocks]


def place_rows_kernel(blocks, peer_ref, *refs):
    out_ref = refs[blocks]
    for block in range(blocks):

        @pl.when(pl.program_id(0) == block)
        def _(block=block):
            out_ref[...] = refs[block][...].astype(out_ref.dtype)


def place_rows(peers, blocks, dtype, *deps):
    count = len(blocks)
    rows, width = blocks[0].shape
    return pl.pallas_call(
        with_deps(functools.partial(place_rows_kernel, count), count, len(deps), 1),
        grid_spec=pltpu.PrefetchScalarGridSpec(
            num_scalar_prefetch=1,
            grid=(count,),
            in_specs=[pl.BlockSpec((rows, width), lambda j, o: (0, 0))] * count
            + [pl.BlockSpec(memory_space=pl.ANY)] * len(deps),
            out_specs=pl.BlockSpec((rows, width), lambda j, o: (o[j], 0)),
        ),
        out_shape=jax.ShapeDtypeStruct((count * rows, width), dtype),
        compiler_params=pltpu.CompilerParams(
            dimension_semantics=("arbitrary",), vmem_limit_bytes=VMEM_LIMIT
        ),
        cost_estimate=SMALL_COST,
        name="place_rows",
    )(peers, *blocks, *deps)


def project_out_kernel(blocks, parts, peer_ref, attn_ref, *refs):
    w_refs, out_refs = refs[:parts], refs[parts : parts + blocks]
    placed_ref, turned = refs[parts + blocks :]
    rows = out_refs[0].shape[0]

    @pl.when(pl.program_id(0) == 0)
    def _():
        turned[...] = attn_ref[...].T
        for block in range(blocks):
            start = pl.multiple_of(peer_ref[block] * rows, rows)
            placed_ref[block * rows : (block + 1) * rows] = turned[pl.ds(start, rows)]

    weights = jnp.concatenate([w_ref[...] for w_ref in w_refs], axis=1)
    store_blocks(out_refs, dot_nt(placed_ref[...], weights))


def project_out(peers, attn_in, weights, start):
    blocks = peers.shape[0]
    columns, tokens = attn_in.shape
    width = weights.shape[0]
    rows = tokens // blocks
    size = math.gcd(start, columns)
    parts = columns // size

    def part_spec(part):
        return pl.BlockSpec((TILE, size), lambda j, o: (j, start // size + part))

    outs = pl.pallas_call(
        functools.partial(project_out_kernel, blocks, parts),
        grid_spec=pltpu.PrefetchScalarGridSpec(
            num_scalar_prefetch=1,
            grid=(width // TILE,),
            in_specs=[pl.BlockSpec((columns, tokens), lambda j, o: (0, 0))]
            + [part_spec(part) for part in range(parts)],
            out_specs=[pl.BlockSpec((rows, TILE), lambda j, o: (0, j))] * blocks
            + [pl.BlockSpec((tokens, columns), lambda j, o: (0, 0))],
            scratch_shapes=[pltpu.VMEM((tokens, columns), LOW)],
        ),
        out_shape=block_shapes(blocks, rows, width)
        + [jax.ShapeDtypeStruct((tokens, columns), LOW)],
        compiler_params=pltpu.CompilerParams(
            dimension_semantics=("arbitrary",), vmem_limit_bytes=VMEM_LIMIT
        ),
        cost_estimate=pl.CostEstimate(
            flops=3 * tokens * columns * width,
            bytes_accessed=4 * width * columns,
            transcendentals=0,
        ),
        name="project_out",
    )(peers, attn_in, *([weights] * parts))
    return outs[:blocks], outs[blocks]


def mix_back_kernel(blocks, parts, peer_ref, *refs):
    mid_refs, w_refs = refs[:blocks], refs[blocks : blocks + parts]
    out_ref, summed, placed = refs[blocks + parts :]
    rows = mid_refs[0].shape[0]
    mid = jnp.concatenate([mid_ref[...] for mid_ref in mid_refs], axis=0)
    weights = jnp.concatenate([w_ref[...] for w_ref in w_refs], axis=1)
    product = dot_nn(mid, weights)

    @pl.when(pl.program_id(0) == 0)
    def _():
        summed[...] = product

    @pl.when(pl.program_id(0) > 0)
    def _():
        summed[...] += product

    @pl.when(pl.program_id(0) == pl.num_programs(0) - 1)
    def _():
        for block in range(blocks):
            start = pl.multiple_of(peer_ref[block] * rows, rows)
            placed[pl.ds(start, rows)] = summed[block * rows : (block + 1) * rows].astype(LOW)
        out_ref[...] = placed[...].T


def mix_back(peers, mid_blocks, weights, start, columns):
    blocks = len(mid_blocks)
    rows, width = mid_blocks[0].shape
    tokens = rows * blocks
    depth = 2 * TILE
    size = math.gcd(start, columns)
    parts = columns // size

    def part_spec(part):
        return pl.BlockSpec((depth, size), lambda j, o: (j, start // size + part))

    return pl.pallas_call(
        functools.partial(mix_back_kernel, blocks, parts),
        grid_spec=pltpu.PrefetchScalarGridSpec(
            num_scalar_prefetch=1,
            grid=(width // depth,),
            in_specs=[pl.BlockSpec((rows, depth), lambda j, o: (0, j))] * blocks
            + [part_spec(part) for part in range(parts)],
            out_specs=pl.BlockSpec((columns, tokens), lambda j, o: (0, 0)),
            scratch_shapes=[pltpu.VMEM((tokens, columns), F32), pltpu.VMEM((tokens, columns), LOW)],
        ),
        out_shape=jax.ShapeDtypeStruct((columns, tokens), LOW),
        compiler_params=pltpu.CompilerParams(
            dimension_semantics=("arbitrary",), vmem_limit_bytes=VMEM_LIMIT
        ),
        cost_estimate=pl.CostEstimate(
            flops=3 * tokens * columns * width,
            bytes_accessed=4 * width * columns,
            transcendentals=0,
        ),
        name="mix_back",
    )(peers, *mid_blocks, *([weights] * parts))


def is_square():
    return lax.axis_size("dp") == 2 and lax.axis_size("ctx") == 4


def swap_core(values):
    return lax.ppermute(values, "ctx", flip_pairs(4, 1))


def swap_across(values):
    return lax.ppermute(values, "ctx", flip_pairs(4, 2))


def swap_along(values):
    return lax.ppermute(values, "dp", flip_pairs(2, 1))


def owner_order(core_flip, across_first):
    along, ctx = lax.axis_index("dp"), lax.axis_index("ctx")
    order = []
    for block in range(4):
        high, low = block >> 1, block & 1
        flip_x, flip_y = (high, low) if across_first else (low, high)
        order.append(((along ^ flip_y) << 2) | (ctx ^ (flip_x << 1) ^ core_flip))
    return jnp.stack(order).astype(jnp.int32)


def travel_open(left_blocks, right, turned, across_first, name, *deps):
    far = row_grads(
        left_blocks, right, turned, owner_order(1, across_first), None, name + "_far", *deps
    )[0]
    return swap_core(far)


def travel_cross(left_blocks, right, turned, across_first, got, name, *deps):
    kept, sent = row_grads(
        left_blocks, right, turned, owner_order(0, across_first), got, name + "_near", *deps
    )
    swap = swap_across if across_first else swap_along
    return kept, swap(sent)


def travel_last(kept, got, across_first):
    swap = swap_along if across_first else swap_across
    total = kept + got.astype(F32)
    return [total[0], swap(total[1].astype(LOW))]


def small_grads_kernel(one_ref, mid_ref, d_projected_ref, attn_ref, grads_ref):
    split = d_projected_ref.shape[0]
    grads_ref[:, :split] = dot_nt(one_ref[...].T, d_projected_ref[...]).astype(LOW)
    grads_ref[:, split:] = dot_nn(mid_ref[...].T, attn_ref[...]).astype(LOW)


def small_grads(normed_one, d_mid_low, d_projected, attn_in):
    tokens, width = normed_one.shape
    columns = d_projected.shape[0] + attn_in.shape[1]
    return tile_call(
        small_grads_kernel,
        "small_grads",
        width // TILE,
        [pl.BlockSpec((tokens, TILE), lambda j: (0, j))] * 2
        + [whole(d_projected.shape), whole(attn_in.shape)],
        [pl.BlockSpec((TILE, columns), lambda j: (j, 0))],
        [jax.ShapeDtypeStruct((width, columns), LOW)],
        2 * tokens * width * columns,
    )(normed_one, d_mid_low, d_projected, attn_in)[0]


def adamw_kernel(turned, step_rate, w_ref, first_ref, second_ref, *refs):
    grad_refs, out_refs, mark_ref = refs[:-4], refs[-4:-1], refs[-1]
    mark_ref[...] = jnp.zeros_like(mark_ref)
    gradient = grad_refs[0][...].astype(F32)
    for grad_ref in grad_refs[1:]:
        gradient = gradient + grad_ref[...].astype(F32)
    if turned:
        gradient = gradient.T
    results = adamw_step(
        w_ref[...], first_ref[...], second_ref[...], gradient, step_rate, WEIGHT_DECAY
    )
    for out_ref, result in zip(out_refs, results):
        out_ref[...] = result


def adamw_call(weight, first, second, terms, start, turned, step_rate, name, *deps):
    rows, columns = weight.shape
    long = rows if turned else columns
    size = math.gcd(math.gcd(start, long), 512)
    if turned:
        spec = pl.BlockSpec((size, columns), lambda j: (j, 0))
    else:
        spec = pl.BlockSpec((rows, size), lambda j: (0, j))
    grad_specs = [
        pl.BlockSpec((term.shape[0], size), lambda j: (0, j + start // size)) for term in terms
    ]
    return tile_call(
        functools.partial(adamw_kernel, turned, step_rate),
        name,
        long // size,
        [spec, spec, spec] + grad_specs,
        [spec] * 3 + [whole((8, 128))],
        [jax.ShapeDtypeStruct(weight.shape, F32)] * 3 + [jax.ShapeDtypeStruct((8, 128), F32)],
        20 * weight.size,
        deps=len(deps),
    )(weight, first, second, *terms, *deps)


def local(
    hidden_in,
    positions,
    cotangent,
    w_qkv,
    w_qkv_first,
    w_qkv_second,
    w_out,
    w_out_first,
    w_out_second,
    w_gate_up,
    w_gate_up_first,
    w_gate_up_second,
    w_down,
    w_down_first,
    w_down_second,
    norm_gains,
    norm_gains_first,
    norm_gains_second,
):
    tensor_count = lax.axis_size("tensor")
    tensor_here = lax.axis_index("tensor")
    ctx_here = lax.axis_index("ctx")
    heads_here = HQ // tensor_count
    kv_here = KV // tensor_count
    head_ratio = HQ // KV
    units_here = FF // tensor_count
    q_cols = heads_here * HD
    k_cols = kv_here * HD
    tok_rows = hidden_in.shape[1]
    seq_rows = positions.shape[1]
    own_rows = tok_rows // tensor_count
    place_row = positions[0]
    query_places = lax.dynamic_slice_in_dim(place_row, ctx_here * tok_rows, tok_rows)
    run_ranks = place_row[::RUN] // RUN
    runs = seq_rows // RUN
    order = jnp.sum(
        jnp.where(
            run_ranks[None, :] == jnp.arange(runs, dtype=jnp.int32)[:, None],
            jnp.arange(runs, dtype=jnp.int32)[None, :],
            0,
        ),
        axis=1,
    ).astype(jnp.int32)
    query_ranks = query_places[::RUN] // RUN

    small_shard = jnp.concatenate([w_qkv.astype(LOW), w_out.astype(LOW).T], axis=1)
    full_small = lax.all_gather(small_shard, ("dp", "ctx"), axis=0, tiled=True)
    full_qkv = full_small[:, : q_cols + 2 * k_cols]
    ffn_shard = jnp.concatenate([w_gate_up.astype(LOW), w_down.astype(LOW).T], axis=1)
    full_ffn = lax.all_gather(ffn_shard, ("dp", "ctx"), axis=0, tiled=True)
    stacked = spread(spread(norm_gains.astype(LOW).astype(F32)[None], "ctx"), "dp")
    gain_values = jnp.swapaxes(stacked, 0, 1).reshape(norm_gains.shape[0], -1)

    hidden = hidden_in[0]
    grad_top = cotangent[0]
    own_start = tensor_here * own_rows
    hidden_own = lax.dynamic_slice_in_dim(hidden, own_start, own_rows).astype(F32)
    grad_own = lax.dynamic_slice_in_dim(grad_top, own_start, own_rows).astype(F32)

    x_hat_one, factor_one = normalize(hidden.astype(F32))
    normed_one = (x_hat_one * gain_values[0]).astype(LOW)
    projected = contract(full_qkv, normed_one, 0, 1)
    cosine, sine = rotary_tables(query_places)
    queries = (
        rotate(projected[:q_cols].reshape(kv_here, head_ratio, HD, tok_rows), cosine, sine)
        * SCORE_SCALE
    ).astype(LOW)
    keys_here = rotate(
        projected[q_cols : q_cols + k_cols].reshape(kv_here, HD, tok_rows), cosine, sine
    ).astype(LOW)
    values_here = projected[q_cols + k_cols :].reshape(kv_here, HD, tok_rows).astype(LOW)
    kv_local = jnp.concatenate([keys_here, values_here], axis=1)
    ctx_peers, tensor_peers = axis_peers("ctx"), axis_peers("tensor")
    kv_blocks = gather_blocks(kv_local, "ctx")
    mixed, attn_low, log_total = attend_forward(order, query_ranks, ctx_peers, queries, kv_blocks)

    def from_here(values, axis=0):
        return blocks_from_here(tensor_count, tensor_here, own_rows, values, axis)

    grad_top = from_here(grad_top)
    out_start = q_cols + 2 * k_cols
    out_parts, attn_in = project_out(
        tensor_peers, attn_low.reshape(q_cols, tok_rows), full_small, out_start
    )
    middle = hidden_own + sum_scatter(out_parts, "tensor")
    x_hat_two, factor_two = normalize(middle)
    normed_two = gather_blocks((x_hat_two * gain_values[1]).astype(LOW), "tensor")
    active, d_gate, d_up, d_two_parts = ffn_both(normed_two, grad_top, full_ffn)
    d_two_pieces = scatter_begin(d_two_parts, "tensor")
    ffn_parts = list(ffn_out(tensor_count, active, full_ffn, d_two_parts[0]))
    d_two_pieces[2], ffn_parts[0] = lax.optimization_barrier((d_two_pieces[2], ffn_parts[0]))
    d_two_pieces = scatter_middle(d_two_pieces, "tensor")
    grad_ffn, mark = ffn_grads(normed_two, grad_top, active, d_gate, d_up, ffn_parts[0])
    d_two_pieces[1:], mark = lax.optimization_barrier((d_two_pieces[1:], mark))
    grad_ffn = held_until(grad_ffn, d_two_pieces[-1])
    red_ffn = lax.optimization_barrier(
        lax.psum_scatter(grad_ffn, ("dp", "ctx"), scatter_dimension=0, tiled=True)
    )
    d_normed_two = scatter_end(d_two_pieces)

    grad_gain_two = jnp.sum(d_normed_two * x_hat_two, axis=0)
    d_middle = grad_own + norm_back(d_normed_two * gain_values[1], x_hat_two, factor_two)
    d_mid_blocks = gather_blocks(d_middle.astype(LOW), "tensor")
    d_mixed = mix_back(tensor_peers, d_mid_blocks, full_small, out_start, q_cols).reshape(
        kv_here, head_ratio, HD, tok_rows
    )
    mark, ffn_parts = lax.optimization_barrier((d_mid_blocks[3:], ffn_parts))
    ffn_pieces = scatter_begin(ffn_parts, "tensor")
    d_query, kv_terms = [], []
    for group in range(kv_here):
        d_heads, *kv_terms = attend_backward(
            group, order, query_ranks, ctx_peers, kv_blocks, kv_terms, queries, d_mixed, mixed,
            log_total, cosine, sine, *mark,
        )
        if group == 0:
            kv_terms, ffn_pieces[1:3] = lax.optimization_barrier((kv_terms, ffn_pieces[1:3]))
            ffn_pieces = scatter_middle(ffn_pieces, "tensor")
        d_query.append(d_heads.reshape(-1, tok_rows))
    kv_terms, ffn_pieces = lax.optimization_barrier((kv_terms, ffn_pieces))
    kv_pieces = scatter_begin(kv_terms, "ctx")
    if is_square():
        out_got = travel_open(d_mid_blocks, attn_in, False, True, "grads_out", kv_terms[0])
    block_own = (middle + scatter_end(ffn_pieces)).astype(LOW)
    if tensor_count == 4:
        block_far = lax.ppermute(block_own, "tensor", flip_pairs(4, 2))
        block_near = lax.ppermute(block_own, "tensor", flip_pairs(4, 1))
    else:
        block_blocks = gather_blocks(block_own, "tensor")

    kv_pieces = scatter_middle(kv_pieces, "ctx")
    if tensor_count == 4:
        kv_pieces[-1], block_far, block_near = lax.optimization_barrier(
            (kv_pieces[-1], block_far, block_near)
        )
    d_one_parts, d_projected = project_back(
        tensor_peers, d_query, kv_pieces, cosine, sine, full_small
    )
    d_one_pieces = scatter_begin(d_one_parts, "tensor")
    adamw_down = functools.partial(
        adamw_call, w_down, w_down_first, w_down_second, [red_ffn], 2 * units_here, True,
        LEARN_RATE, "adamw_down",
    )
    adamw_gate_up = functools.partial(
        adamw_call, w_gate_up, w_gate_up_first, w_gate_up_second, [red_ffn], 0, False,
        LEARN_RATE, "adamw_gate_up",
    )
    if is_square():
        out_kept, out_got = travel_cross(
            d_mid_blocks, attn_in, False, True, out_got, "grads_out", d_one_parts[0]
        )
        d_one_pieces[2], out_kept = lax.optimization_barrier((d_one_pieces[2], out_kept))
        d_one_pieces = scatter_middle(d_one_pieces, "tensor")
        qkv_far = row_grads(
            [normed_one], d_projected, True, owner_order(1, False), None, "grads_qkv_far", out_kept
        )[0]
        d_one_pieces[1:], out_kept, qkv_far = lax.optimization_barrier(
            (d_one_pieces[1:], out_kept, qkv_far)
        )
        qkv_got = swap_core(qkv_far)
    else:
        grad_small = small_grads(
            normed_one, jnp.concatenate(d_mid_blocks, axis=0), d_projected, attn_in
        )
        d_one_pieces = scatter_middle(d_one_pieces, "tensor")
        red_small = lax.optimization_barrier(
            lax.psum_scatter(grad_small, ("dp", "ctx"), scatter_dimension=0, tiled=True)
        )
    d_normed_one = scatter_end(d_one_pieces)
    x_hat_own, factor_own = normalize(hidden_own)
    grad_gain_one = jnp.sum(d_normed_one * x_hat_own, axis=0)
    grad_in_own = d_middle + norm_back(d_normed_one * gain_values[0], x_hat_own, factor_own)
    grad_in_low = grad_in_own.astype(LOW)
    gain_rows = jnp.stack([grad_gain_one, grad_gain_two])
    if is_square():
        qkv_kept, qkv_got = travel_cross(
            [normed_one], d_projected, True, False, qkv_got, "grads_qkv"
        )
    gu_first, gu_second, gu_new, mark = adamw_gate_up(d_normed_one)
    if tensor_count == 4:
        near = lax.ppermute(grad_in_low, "tensor", flip_pairs(4, 1))
        far = lax.ppermute(grad_in_low, "tensor", flip_pairs(4, 2))
        near, far, mark, gain_rows, block_far = lax.optimization_barrier(
            (near, far, mark, gain_rows, block_far)
        )
        if is_square():
            near, out_got, qkv_kept = lax.optimization_barrier((near, out_got, qkv_kept))
        grad_in_blocks = [grad_in_low, near, far, lax.ppermute(far, "tensor", flip_pairs(4, 1))]
        block_last = lax.ppermute(block_far, "tensor", flip_pairs(4, 1))
        block_blocks = [block_own, block_near, block_far, block_last]
    else:
        grad_in_blocks = gather_blocks(grad_in_low, "tensor")
    small_start = 0
    if not is_square():
        small_start, out_terms, qkv_terms = out_start, [red_small], [red_small]
    else:
        out_terms = travel_last(out_kept, out_got, True)
        qkv_terms = travel_last(qkv_kept, qkv_got, False)
    down_first, down_second, down_new, mark = adamw_down(mark)
    out_first, out_second, out_new, mark = adamw_call(
        w_out, w_out_first, w_out_second, out_terms, small_start, True, OUT_RATE, "adamw_out", mark
    )
    gain_sums = sum_everywhere(gain_rows, "tensor")
    gain_parts = jnp.swapaxes(gain_sums.reshape(2, -1, norm_gains.shape[1]), 0, 1)
    red_gains = gains_scatter(gains_scatter(gain_parts, "dp"), "ctx")[0]
    grad_in_blocks[3], red_gains = lax.optimization_barrier((grad_in_blocks[3], red_gains))
    qkv_first, qkv_second, qkv_new, last_mark = adamw_call(
        w_qkv, w_qkv_first, w_qkv_second, qkv_terms, 0, False, LEARN_RATE, "adamw_qkv", mark
    )
    grad_in = place_rows(tensor_peers, grad_in_blocks, F32, block_blocks[3], mark)
    grad_in = grad_in.reshape(hidden_in.shape)
    block_out = place_rows(tensor_peers, block_blocks, LOW).reshape(hidden_in.shape)
    gain_first, gain_second, gain_new = adamw_step(
        norm_gains, norm_gains_first, norm_gains_second, red_gains, GAIN_RATE, 0.0
    )
    return (
        block_out,
        grad_in,
        qkv_first,
        qkv_second,
        qkv_new,
        out_first,
        out_second,
        out_new,
        gu_first,
        gu_second,
        gu_new,
        down_first,
        down_second,
        down_new,
        gain_first,
        gain_second,
        gain_new,
    )


def solution(mesh):
    tokens = P("dp", "ctx", None)
    rows = P(("dp", "ctx"), "tensor")
    columns = P("tensor", ("dp", "ctx"))
    gains = P(None, ("dp", "ctx"))
    placed = (
        (tokens, P("dp", None), tokens)
        + (rows,) * 3
        + (columns,) * 3
        + (rows,) * 3
        + (columns,) * 3
        + (gains,) * 3
    )
    return jax.shard_map(
        local,
        mesh=mesh,
        in_specs=placed,
        out_specs=(tokens, tokens) + placed[3:],
        check_vma=False,
    )
```

time: 1540 us -> 498 us (0.32)
  waiting for transfers between devices: 1190 us -> 202 us
  matrix products: 208 us -> 3.75 us
  Pallas kernels: 0 us -> 164 us
  other arithmetic: 84.4 us -> 27.8 us
  starting transfers between devices: 1.75 us -> 56 us
    psum x3 -> x0, waiting for transfers between devices: 588 us -> none  [the longest x1 285 us: local(): lax.psum(jnp.dot(activated, full_down, preferred_element_type=jnp.float32...]
    reduce_scatter x5 -> x1, waiting for transfers between devices: 413 us -> 0.02 us  [local(): lax.psum_scatter(grad_ffn, ('dp', 'ctx'), scatter_dimension=0, tiled=True)]
    ppermute x0 -> x47, waiting for transfers between devices: none -> 168 us  [the longest x4 44 us: gather_blocks(): far = lax.ppermute(rows, axis, flip_pairs(count, 2))]
    pallas_call x0 -> x20, Pallas kernels: none -> 164 us  [the longest x1 32.5 us: ffn_both(): tile_call(functools.partial(ffn_both_kernel, blocks, tiles), 'ffn_both',...]
    dot_general x18 -> x0, matrix products: 131 us -> none  [the longest x4 23.4 us: block_scores(): jnp.einsum('qgrd,kgd->grqk', queries, key_block, preferred_element_type=j...]
    all_gather x5 -> x2, waiting for transfers between devices: 163 us -> 33.6 us  [the longest x1 24.6 us: local(): full_small = lax.all_gather(small_shard, ('dp', 'ctx'), axis=0, tiled=True)]
    dot_general x8 -> x1, matrix products: 76.7 us -> 3.75 us  [contract(): lax.dot_general(left, right, (((left_dim,), (right_dim,)), ((), ())), pre...]
    ppermute x0 -> x47, starting transfers between devices: none -> 55.9 us  [the longest x5 9.97 us: scatter_middle(): lax.ppermute(joined, axis, flip_pairs(count, 2))]
  transfers between devices with their start and end apart: 14 -> 50, of which waited for: 13 -> 29; matrix products, arithmetic and copies ran while one was open for 11% -> 7% of each run, Pallas kernels for 0% -> 25%
where the time goes in v1:
time: 498 us; the launch traced here: 495 us
  waiting for transfers between devices  202 us (41%)
  Pallas kernels  164 us (33%)
  starting transfers between devices  56 us (11%)
  other arithmetic  27.8 us (6%)
  local copies, waits for them, and re-layouts  27.5 us (6%)
  between operations  14.9 us (3%)
    ppermute x4, waiting for transfers between devices, gather_blocks(): far = lax.ppermute(rows, axis, flip_pairs(count, 2))  44 us
    ppermute x5, waiting for transfers between devices, scatter_middle(): lax.ppermute(near, axis, flip_pairs(count, 1))  40.5 us
    pallas_call x1, Pallas kernels, ffn_both(): tile_call(functools.partial(ffn_both_kernel, blocks, tiles), 'ffn_both',...  32.5 us
    ppermute x5, waiting for transfers between devices, scatter_middle(): lax.ppermute(joined, axis, flip_pairs(count, 2))  25.3 us
    all_gather x1, waiting for transfers between devices, local(): full_small = lax.all_gather(small_shard, ('dp', 'ctx'), axis=0, tiled=True)  24.6 us
    unnamed x172, local copies, waits for them, and re-layouts  24 us
    pallas_call x2, Pallas kernels, attend_backward(): pl.pallas_call(with_deps(functools.partial(backward_kernel, devices, per_...  21.6 us
    pallas_call x4, Pallas kernels, adamw_call(): tile_call(functools.partial(adamw_kernel, turned, step_rate), name, long...  21.5 us
  transfers between devices with their start and end apart: 50, of which 29 were waited for; matrix products, arithmetic and copies ran while one was open for 7% of the time, Pallas kernels for 25%

profile of v1, /device:TPU:0, one launch (start us, length us, event | category | flops | bytes accessed | tf_op | source)
XLA Modules:
  0.0 495.4 jit_solution(16423497141694636533)
XLA Ops:
  30.2 24.6 %all-gather.3.cloned.1.call-done.refs_0_.refs_1_.refs_4_.refs_5_.refs_8_ = bf16[2048,1280]{1,0:T(8,128)(2,1)} async-done(((bf16[256,1280]{1,0:T(8,128)(2,1)}), bf16[2048,1280]{1,0:T(8,128)(2,1)}) %all-gather.3.cloned.1.call-update) | async-done | bytes 5242896 | tf_op jit(solution)/shard_map/all_gather | solution.py:1058
  60.4 6.8 %collective-permute-done.5.refs_2_.refs_5_ = bf16[2,128,512]{2,1,0:T(8,128)(2,1)S(1)} collective-permute-done((bf16[2,128,512]{2,1,0:T(8,128)(2,1)S(1)}, bf16[2,128,512]{2,1,0:T(8,128)(2,1)S(1)}, u32[]{:S(2)}, u32[]{:S(2)}) %collective-permute-start.5) | collective-permute-done | bytes 262176 | tf_op jit(solution)/shard_map/ppermute | solution.py:167
  68.8 14.6 %attend_forward.1 = (f32[2,4,64,512]{3,2,1,0:T(8,128)S(1)}, bf16[2,4,64,512]{3,2,1,0:T(8,128)(2,1)S(1)}, f32[2,4,1,512]{3,2,1,0:T(1,128)S(1)}) custom-call(s32[8]{0:T(128)S(1)} %select_reduce_fusion.order_ref.refs_0_, s32[2]{0:T(128)S(1)} %and_select_fusion.rank_ref.refs_1_, s32[4]{0:T(128)S(1)} %pad_add_fusion.1.peer_ref.refs_2_, ...), custom_call_target="tpu_custom_call" | custom-call | flops 34359738368 | bytes 8388608 | tf_op jit(solution)/shard_map/attend_forward/pallas_call | solution.py:347
  85.1 7.4 %project_out.1 = (f32[128,2048]{1,0:T(8,128)S(1)}, bf16[128,2048]{1,0:T(8,128)(2,1)}, f32[128,2048]{1,0:T(8,128)S(1)}, bf16[128,2048]{1,0:T(8,128)(2,1)S(1)}, bf16[512,512]{1,0:T(8,128)(2,1)S(1)}) custom-call(s32[4]{0:T(128)S(1)} %pad_add_fusion.peer_ref.refs_0_, bf16[512,512]{1,0:T(8,128)(2,1)S(1)} %bitcast.82, ...), custom_call_target="tpu_custom_call" | custom-call | flops 1610612736 | bytes 4194304 | tf_op jit(solution)/shard_map/project_out/pallas_call | solution.py:821
  94.8 12.5 %collective-permute-done.7 = bf16[128,2048]{1,0:T(8,128)(2,1)S(1)} collective-permute-done((bf16[128,2048]{1,0:T(8,128)(2,1)S(1)}, bf16[128,2048]{1,0:T(8,128)(2,1)S(1)}, u32[]{:S(2)}, u32[]{:S(2)}) %collective-permute-start.7) | collective-permute-done | bytes 524320 | tf_op jit(solution)/shard_map/ppermute | solution.py:96
  112.1 18.8 %collective-permute-done.8 = bf16[128,2048]{1,0:T(8,128)(2,1)} collective-permute-done((bf16[128,2048]{1,0:T(8,128)(2,1)}, bf16[128,2048]{1,0:T(8,128)(2,1)}, u32[]{:S(2)}, u32[]{:S(2)}) %collective-permute-start.8) | collective-permute-done | bytes 524320 | tf_op jit(solution)/shard_map/ppermute | solution.py:112
  130.9 4.2 collective-permute-done.9
  141.8 18.3 %collective-permute-done.11.refs_2_ = bf16[128,2048]{1,0:T(8,128)(2,1)S(1)} collective-permute-done((bf16[128,2048]{1,0:T(8,128)(2,1)S(1)}, bf16[128,2048]{1,0:T(8,128)(2,1)S(1)}, u32[]{:S(2)}, u32[]{:S(2)}) %collective-permute-start.11) | collective-permute-done | bytes 524320 | tf_op jit(solution)/shard_map/ppermute | solution.py:167
  165.2 7.6 %collective-permute-done.12.refs_3_ = bf16[128,2048]{1,0:T(8,128)(2,1)S(1)} collective-permute-done((bf16[128,2048]{1,0:T(8,128)(2,1)S(1)}, bf16[128,2048]{1,0:T(8,128)(2,1)S(1)}, u32[]{:S(2)}, u32[]{:S(2)}) %collective-permute-start.12) | collective-permute-done | bytes 524320 | tf_op jit(solution)/shard_map/ppermute | solution.py:169
  173.6 9.0 %all-gather.5.cloned.1.call-done.refs_5_.refs_6_.refs_7_.refs_8_.refs_9_.refs_1_ = bf16[2048,6144]{1,0:T(8,128)(2,1)} async-done(((bf16[256,6144]{1,0:T(8,128)(2,1)}), bf16[2048,6144]{1,0:T(8,128)(2,1)}) %all-gather.5.cloned.1.call-update) | async-done | bytes 25165840 | tf_op jit(solution)/shard_map/all_gather | solution.py:1061
  185.7 32.5 %ffn_both.1 = (bf16[512,2048]{1,0:T(8,128)(2,1)}, bf16[512,2048]{1,0:T(8,128)(2,1)}, bf16[512,2048]{1,0:T(8,128)(2,1)}, f32[128,2048]{1,0:T(8,128)S(1)}, bf16[12...) custom-call(bf16[128,2048]{1,0:T(8,128)(2,1)S(1)} %copy-done.19, ...), custom_call_target="tpu_custom_call" | custom-call | flops 32212254720 | bytes 18874368 | tf_op jit(solution)/shard_map/ffn_both/pallas_call | solution.py:560
  219.7 9.8 %ffn_out.1 = (f32[128,2048]{1,0:T(8,128)S(1)}, bf16[128,2048]{1,0:T(8,128)(2,1)S(1)}, f32[128,2048]{1,0:T(8,128)S(1)}, bf16[128,2048]{1,0:T(8,128)(2,1)S(1)}) custom-call(bf16[512,2048]{1,0:T(8,128)(2,1)} %get-tuple-element.147.refs_0_.refs_5_, bf16[2048,6144]{1,0:T(8,128)(2,1)} %all-gather.5.cloned.1.call-done.refs_5_.refs_6_.refs_7_.refs_8_.refs_9_.refs_1_, ...), custom_call_target="tpu_custom_call" | custom-call | flops 6442450944 | bytes 6291456 | tf_op jit(solution)/shard_map/ffn_out/pallas_call | solution.py:584
  236.4 19.8 %ffn_grads.1 = (bf16[2048,6144]{1,0:T(8,128)(2,1)}, f32[8,128]{1,0:T(8,128)}) custom-call(bf16[128,2048]{1,0:T(8,128)(2,1)S(1)} %copy-done.19, bf16[128,2048]{1,0:T(8,128)(2,1)} %collective-permute-done.10.refs_1_, bf16[128,2048]{1,0:T(8,128)(2,1)S(1)} %copy-done.36, bf16[128,2048]{1,0:T(8,128)(2,1)S(1)} %copy-done.39, bf16[512,2048]{1,0:T(8,128)(2,1)S(1)} %copy-done.2, ...), custom_call_target="tpu_custom_call" | custom-call | flops 19327352832 | bytes 50339840 | tf_op jit(solution)/shard_map/ffn_grads/pallas_call | solution.py:611
  268.9 18.9 %collective-permute-done.17.refs_2_.refs_3_ = bf16[128,2048]{1,0:T(8,128)(2,1)S(1)} collective-permute-done((bf16[128,2048]{1,0:T(8,128)(2,1)S(1)}, bf16[128,2048]{1,0:T(8,128)(2,1)S(1)}, u32[]{:S(2)}, u32[]{:S(2)}) %collective-permute-start.17) | collective-permute-done | bytes 524320 | tf_op jit(solution)/shard_map/ppermute | solution.py:167
  288.9 11.4 %collective-permute-done.18.refs_3_.refs_13_.refs_17_.refs_4_ = bf16[128,2048]{1,0:T(8,128)(2,1)} collective-permute-done((bf16[128,2048]{1,0:T(8,128)(2,1)S(1)}, bf16[128,2048]{1,0:T(8,128)(2,1)}, u32[]{:S(2)}, u32[]{:S(2)}) %collective-permute-start.18) | collective-permute-done | bytes 524320 | tf_op jit(solution)/shard_map/ppermute | solution.py:169
  302.0 5.0 %mix_back.1 = bf16[512,512]{1,0:T(8,128)(2,1)S(1)} custom-call(s32[4]{0:T(128)S(1)} %pad_add_fusion.peer_ref.refs_0_, bf16[128,2048]{1,0:T(8,128)(2,1)S(1)} %copy-done.4, bf16[128,2048]{1,0:T(8,128)(2,1)S(1)} %collective-permute-done.16.refs_1_.refs_2_, bf16[128,2048]{1,0:T(8,128)(2,1)S(1)} %collective-permute-done.17.refs_2_.refs_3_, ...), custom_call_target="tpu_custom_call" | custom-call | flops 1610612736 | bytes 4194304 | tf_op jit(solution)/shard_map/mix_back/pallas_call | solution.py:882
  307.1 10.9 %attend_backward.2 = (bf16[1,4,64,512]{3,2,1,0:T(8,128)(2,1)S(1)}, bf16[128,512]{1,0:T(8,128)(2,1)S(1)}, bf16[128,512]{1,0:T(8,128)(2,1)S(1)}, bf16[128,512]{1,0:T(8,128)(2,1)S(1)}, bf16[128,512]{1,0:T(8,128)(2,1)S(1)}) custom-call(s32[8]{0:T(128)S(1)} %select_reduce_fusion.order_ref.refs_0_, s32[2]{0:T(128)S(1)} %and_select_fusion.rank_ref.refs_1_, ...), custom_call_target="tpu_custom_call" | custom-call | flops 34359738368 | bytes 8388608 | tf_op jit(solution)/shard_map/attend_backward/pallas_call | solution.py:397
  322.5 10.7 %attend_backward.3 = (bf16[1,4,64,512]{3,2,1,0:T(8,128)(2,1)S(1)}, bf16[256,512]{1,0:T(8,128)(2,1)S(1)}, bf16[256,512]{1,0:T(8,128)(2,1)S(1)}, bf16[256,512]{1,0:T(8,128)(2,1)S(1)}, bf16[256,512]{1,0:T(8,128)(2,1)S(1)}) custom-call(s32[8]{0:T(128)S(1)} %select_reduce_fusion.order_ref.refs_0_, s32[2]{0:T(128)S(1)} %and_select_fusion.rank_ref.refs_1_, ...), custom_call_target="tpu_custom_call" | custom-call | flops 34359738368 | bytes 8388608 | tf_op jit(solution)/shard_map/attend_backward/pallas_call | solution.py:397
  333.2 7.0 %collective-permute-done.20 = bf16[128,2048]{1,0:T(8,128)(2,1)S(1)} collective-permute-done((bf16[128,2048]{1,0:T(8,128)(2,1)S(1)}, bf16[128,2048]{1,0:T(8,128)(2,1)S(1)}, u32[]{:S(2)}, u32[]{:S(2)}) %collective-permute-start.20) | collective-permute-done | bytes 524320 | tf_op jit(solution)/shard_map/ppermute | solution.py:112
  340.5 4.9 collective-permute-start.25
  348.4 4.4 grads_out_far.1
  353.5 14.0 %collective-permute-done.23.refs_5_ = bf16[256,512]{1,0:T(8,128)(2,1)S(1)} collective-permute-done((bf16[256,512]{1,0:T(8,128)(2,1)S(1)}, bf16[256,512]{1,0:T(8,128)(2,1)S(1)}, u32[]{:S(2)}, u32[]{:S(2)}) %collective-permute-start.23) | collective-permute-done | bytes 262176 | tf_op jit(solution)/shard_map/ppermute | solution.py:113
  372.7 8.0 %project_back.1 = (f32[128,2048]{1,0:T(8,128)S(1)}, bf16[128,2048]{1,0:T(8,128)(2,1)S(1)}, f32[128,2048]{1,0:T(8,128)S(1)}, bf16[128,2048]{1,0:T(8,128)(2,1)}, bf16[768,512]{1,0:T(8,128)(2,1)S(1)}) custom-call(s32[4]{0:T(128)S(1)} %pad_add_fusion.peer_ref.refs_0_, bf16[256,512]{1,0:T(8,128)(2,1)S(1)} %bitcast.83, bf16[256,512]{1,0:T(8,128)(2,1)S(1)} %bitcast.84, ...), custom_call_target="tpu_custom_call" | custom-call | flops 1000 | bytes 1000 | tf_op jit(solution)/shard_map/project_back/pallas_call | solution.py:733
  386.8 4.6 grads_out_near.1
  391.4 5.5 %collective-permute-done.27 = bf16[128,2048]{1,0:T(8,128)(2,1)} collective-permute-done((bf16[128,2048]{1,0:T(8,128)(2,1)}, bf16[128,2048]{1,0:T(8,128)(2,1)}, u32[]{:S(2)}, u32[]{:S(2)}) %collective-permute-start.27) | collective-permute-done | bytes 524320 | tf_op jit(solution)/shard_map/ppermute | solution.py:96
  405.0 14.5 %collective-permute-done.29 = bf16[128,2048]{1,0:T(8,128)(2,1)S(1)} collective-permute-done((bf16[128,2048]{1,0:T(8,128)(2,1)S(1)}, bf16[128,2048]{1,0:T(8,128)(2,1)S(1)}, u32[]{:S(2)}, u32[]{:S(2)}) %collective-permute-start.29) | collective-permute-done | bytes 524320 | tf_op jit(solution)/shard_map/ppermute | solution.py:112
  419.5 5.1 %collective-permute-done.30 = bf16[128,2048]{1,0:T(8,128)(2,1)S(1)} collective-permute-done((bf16[128,2048]{1,0:T(8,128)(2,1)S(1)}, bf16[128,2048]{1,0:T(8,128)(2,1)S(1)}, u32[]{:S(2)}, u32[]{:S(2)}) %collective-permute-start.30) | collective-permute-done | bytes 524320 | tf_op jit(solution)/shard_map/ppermute | solution.py:113
  428.8 4.6 grads_qkv_near.1
  435.4 11.8 %adamw_gate_up.1 = (f32[256,4096]{1,0:T(8,128)}, f32[256,4096]{1,0:T(8,128)}, f32[256,4096]{1,0:T(8,128)}, f32[8,128]{1,0:T(8,128)S(1)}) custom-call(f32[256,4096]{1,0:T(8,128)} %refs_0_.4, f32[256,4096]{1,0:T(8,128)} %refs_1_.4, f32[256,4096]{1,0:T(8,128)} %refs_2_.4, bf16[256,6144]{1,0:T(8,128)(2,1)S(1)} %copy-done.1, ...), custom_call_target="tpu_custom_call" | custom-call | flops 31457280 | bytes 25174016 | tf_op jit(solution)/shard_map/adamw_gate_up/pallas_call | solution.py:999
  447.2 4.9 collective-permute-done.32.refs_3_
  469.1 5.9 %adamw_down.1 = (f32[2048,256]{1,0:T(8,128)}, f32[2048,256]{1,0:T(8,128)}, f32[2048,256]{1,0:T(8,128)}, f32[8,128]{1,0:T(8,128)S(1)}) custom-call(f32[2048,256]{1,0:T(8,128)S(1)} %copy-done.7, f32[2048,256]{1,0:T(8,128)S(1)} %copy-done.26, f32[2048,256]{1,0:T(8,128)} %refs_2_.5, bf16[256,6144]{1,0:T(8,128)(2,1)} %reduce-scatter.2.cloned.1.call-done.refs_3_, ...), custom_call_target="tpu_custom_call" | custom-call | flops 15728640 | bytes 12591104 | tf_op jit(solution)/shard_map/adamw_down/pallas_call | solution.py:999
  484.6 4.2 place_rows.3
  (334 shorter events, 138.4 us)
Async XLA Ops:
  7.2 47.6 %all-gather.3.cloned.1.call-start = ((), (), s32[]{:S(2)}) async-start(), calls=%async_computation.1 | async-start | bytes 5898240 | tf_op jit(solution)/shard_map/all_gather | solution.py:1058
  10.7 172.0 %all-gather.5.cloned.1.call-start = ((), (), s32[]{:S(2)}) async-start(), calls=%async_computation.2 | async-start | bytes 28311552 | tf_op jit(solution)/shard_map/all_gather | solution.py:1061
  15.7 417.8 %reduce-scatter.2.cloned.1.call-start = ((), (), s32[]{:S(2)}) async-start(), calls=%async_computation.3 | async-start | bytes 28311552 | tf_op jit(solution)/shard_map/reduce_scatter | solution.py:1108
  93.3 14.0 %collective-permute-start.7 = (bf16[128,2048]{1,0:T(8,128)(2,1)S(1)}, bf16[128,2048]{1,0:T(8,128)(2,1)S(1)}, u32[]{:S(2)}, u32[]{:S(2)}) collective-permute-start(bf16[128,2048]{1,0:T(8,128)(2,1)S(1)} %get-tuple-element.138), channel_id=1, source_target_pairs={{0,1},{1,0},{2,3},{3,2},{4,5},{5,4},{6,7},{7,6},{8,9},{9,8},{10,11... | collective-permute-start | bytes 1572872 | tf_op jit(solution)/shard_map/ppermute | solution.py:96
  107.3 23.6 %collective-permute-start.8 = (bf16[128,2048]{1,0:T(8,128)(2,1)}, bf16[128,2048]{1,0:T(8,128)(2,1)}, u32[]{:S(2)}, u32[]{:S(2)}) collective-permute-start(bf16[128,2048]{1,0:T(8,128)(2,1)} %get-tuple-element.139), channel_id=1, source_target_pairs={{0,1},{1,0},{2,3},{3,2},{4,5},{5,4},{6,7},{7,6},{8,9},{9,8},{10,11... | collective-permute-start | bytes 1572872 | tf_op jit(solution)/shard_map/ppermute | solution.py:112
  109.7 25.4 %collective-permute-start.9 = (bf16[128,2048]{1,0:T(8,128)(2,1)}, bf16[128,2048]{1,0:T(8,128)(2,1)}, u32[]{:S(2)}, u32[]{:S(2)}) collective-permute-start(bf16[128,2048]{1,0:T(8,128)(2,1)} %add_convert_fusion.4), channel_id=1, source_target_pairs={{0,2},{1,3},{2,0},{3,1},{4,6},{5,7},{6,4},{7,5},{8,10},{9,11},{10,... | collective-permute-start | bytes 1572872 | tf_op jit(solution)/shard_map/ppermute | solution.py:113
  138.8 21.3 %collective-permute-start.11 = (bf16[128,2048]{1,0:T(8,128)(2,1)S(1)}, bf16[128,2048]{1,0:T(8,128)(2,1)S(1)}, u32[]{:S(2)}, u32[]{:S(2)}) collective-permute-start(bf16[128,2048]{1,0:T(8,128)(2,1)S(1)} %multiply_convert_fusion.refs_0_), channel_id=1, source_target_pairs={{0,2},{1,3},{2,0},{3,1},{4,6},{5,7},{6,4},{7,5},{8,10},{9,11},{10,... | collective-permute-start | bytes 1572872 | tf_op jit(solution)/shard_map/ppermute | solution.py:167
  138.9 21.4 %collective-permute-start.10 = (bf16[128,2048]{1,0:T(8,128)(2,1)S(1)}, bf16[128,2048]{1,0:T(8,128)(2,1)}, u32[]{:S(2)}, u32[]{:S(2)}) collective-permute-start(bf16[128,2048]{1,0:T(8,128)(2,1)S(1)} %multiply_convert_fusion.refs_0_), channel_id=1, source_target_pairs={{0,1},{1,0},{2,3},{3,2},{4,5},{5,4},{6,7},{7,6},{8,9},{9,8},{10,11... | collective-permute-start | bytes 1572872 | tf_op jit(solution)/shard_map/ppermute | solution.py:166
  160.2 12.6 %collective-permute-start.12 = (bf16[128,2048]{1,0:T(8,128)(2,1)S(1)}, bf16[128,2048]{1,0:T(8,128)(2,1)S(1)}, u32[]{:S(2)}, u32[]{:S(2)}) collective-permute-start(bf16[128,2048]{1,0:T(8,128)(2,1)S(1)} %collective-permute-done.11.refs_2_), channel_id=1, source_target_pairs={{0,1},{1,0},{2,3},{3,2},{4,5},{5,4},{6,7},{7,6},{8,9},{9,8},{10,11... | collective-permute-start | bytes 1572872 | tf_op jit(solution)/shard_map/ppermute | solution.py:169
  218.2 14.1 %collective-permute-start.13 = (bf16[128,2048]{1,0:T(8,128)(2,1)S(1)}, bf16[128,2048]{1,0:T(8,128)(2,1)S(1)}, u32[]{:S(2)}, u32[]{:S(2)}) collective-permute-start(bf16[128,2048]{1,0:T(8,128)(2,1)S(1)} %get-tuple-element.146), channel_id=1, source_target_pairs={{0,1},{1,0},{2,3},{3,2},{4,5},{5,4},{6,7},{7,6},{8,9},{9,8},{10,11... | collective-permute-start | bytes 1572872 | tf_op jit(solution)/shard_map/ppermute | solution.py:96
  232.3 24.1 %collective-permute-start.14 = (bf16[128,2048]{1,0:T(8,128)(2,1)S(1)}, bf16[128,2048]{1,0:T(8,128)(2,1)S(1)}, u32[]{:S(2)}, u32[]{:S(2)}) collective-permute-start(bf16[128,2048]{1,0:T(8,128)(2,1)S(1)} %get-tuple-element.150), channel_id=1, source_target_pairs={{0,1},{1,0},{2,3},{3,2},{4,5},{5,4},{6,7},{7,6},{8,9},{9,8},{10,11... | collective-permute-start | bytes 1572872 | tf_op jit(solution)/shard_map/ppermute | solution.py:112
  233.9 25.3 %collective-permute-start.15 = (bf16[128,2048]{1,0:T(8,128)(2,1)S(1)}, bf16[128,2048]{1,0:T(8,128)(2,1)}, u32[]{:S(2)}, u32[]{:S(2)}) collective-permute-start(bf16[128,2048]{1,0:T(8,128)(2,1)S(1)} %add_convert_fusion.3), channel_id=1, source_target_pairs={{0,2},{1,3},{2,0},{3,1},{4,6},{5,7},{6,4},{7,5},{8,10},{9,11},{10,... | collective-permute-start | bytes 1572872 | tf_op jit(solution)/shard_map/ppermute | solution.py:113
  265.2 22.6 %collective-permute-start.17 = (bf16[128,2048]{1,0:T(8,128)(2,1)S(1)}, bf16[128,2048]{1,0:T(8,128)(2,1)S(1)}, u32[]{:S(2)}, u32[]{:S(2)}) collective-permute-start(bf16[128,2048]{1,0:T(8,128)(2,1)S(1)} %get-tuple-element.253.refs_0_.refs_1_), channel_id=1, source_target_pairs={{0,2},{1,3},{2,0},{3,1},{4,6},{5,7},{6,4},{7,5},{8,10},{9,11},{10,... | collective-permute-start | bytes 1572872 | tf_op jit(solution)/shard_map/ppermute | solution.py:167
  265.3 22.5 %collective-permute-start.16 = (bf16[128,2048]{1,0:T(8,128)(2,1)S(1)}, bf16[128,2048]{1,0:T(8,128)(2,1)S(1)}, u32[]{:S(2)}, u32[]{:S(2)}) collective-permute-start(bf16[128,2048]{1,0:T(8,128)(2,1)S(1)} %get-tuple-element.253.refs_0_.refs_1_), channel_id=1, source_target_pairs={{0,1},{1,0},{2,3},{3,2},{4,5},{5,4},{6,7},{7,6},{8,9},{9,8},{10,11... | collective-permute-start | bytes 1572872 | tf_op jit(solution)/shard_map/ppermute | solution.py:166
  300.3 17.8 %collective-permute-start.19 = (bf16[128,2048]{1,0:T(8,128)(2,1)}, bf16[128,2048]{1,0:T(8,128)(2,1)S(1)}, u32[]{:S(2)}, u32[]{:S(2)}) collective-permute-start(bf16[128,2048]{1,0:T(8,128)(2,1)} %copy-done.50), channel_id=1, source_target_pairs={{0,1},{1,0},{2,3},{3,2},{4,5},{5,4},{6,7},{7,6},{8,9},{9,8},{10,11... | collective-permute-start | bytes 1572872 | tf_op jit(solution)/shard_map/ppermute | solution.py:96
  318.1 22.1 %collective-permute-start.20 = (bf16[128,2048]{1,0:T(8,128)(2,1)S(1)}, bf16[128,2048]{1,0:T(8,128)(2,1)S(1)}, u32[]{:S(2)}, u32[]{:S(2)}) collective-permute-start(bf16[128,2048]{1,0:T(8,128)(2,1)S(1)} %copy-done.49), channel_id=1, source_target_pairs={{0,1},{1,0},{2,3},{3,2},{4,5},{5,4},{6,7},{7,6},{8,9},{9,8},{10,11... | collective-permute-start | bytes 1572872 | tf_op jit(solution)/shard_map/ppermute | solution.py:112
  320.0 20.2 %collective-permute-start.21 = (bf16[128,2048]{1,0:T(8,128)(2,1)S(1)}, bf16[128,2048]{1,0:T(8,128)(2,1)S(1)}, u32[]{:S(2)}, u32[]{:S(2)}) collective-permute-start(bf16[128,2048]{1,0:T(8,128)(2,1)S(1)} %add_convert_fusion.2), channel_id=1, source_target_pairs={{0,2},{1,3},{2,0},{3,1},{4,6},{5,7},{6,4},{7,5},{8,10},{9,11},{10,... | collective-permute-start | bytes 1572872 | tf_op jit(solution)/shard_map/ppermute | solution.py:113
  340.2 12.5 %collective-permute-start.22 = (bf16[256,512]{1,0:T(8,128)(2,1)S(1)}, bf16[256,512]{1,0:T(8,128)(2,1)S(1)}, u32[]{:S(2)}, u32[]{:S(2)}) collective-permute-start(bf16[256,512]{1,0:T(8,128)(2,1)S(1)} %get-tuple-element.189), channel_id=1, source_target_pairs={{0,4},{4,0},{8,12},{12,8},{1,5},{5,1},{9,13},{13,9},{2,6},{6,2},{1... | collective-permute-start | bytes 786440 | tf_op jit(solution)/shard_map/ppermute | solution.py:96
  340.5 28.5 %collective-permute-start.25 = (bf16[128,2048]{1,0:T(8,128)(2,1)S(1)}, bf16[128,2048]{1,0:T(8,128)(2,1)S(1)}, u32[]{:S(2)}, u32[]{:S(2)}) collective-permute-start(bf16[128,2048]{1,0:T(8,128)(2,1)S(1)} %add_convert_fusion.1.refs_1_), channel_id=1, source_target_pairs={{0,1},{1,0},{2,3},{3,2},{4,5},{5,4},{6,7},{7,6},{8,9},{9,8},{10,11... | collective-permute-start | bytes 1572872 | tf_op jit(solution)/shard_map/ppermute | solution.py:1137
  345.4 26.5 %collective-permute-start.24 = (bf16[128,2048]{1,0:T(8,128)(2,1)S(1)}, bf16[128,2048]{1,0:T(8,128)(2,1)S(1)}, u32[]{:S(2)}, u32[]{:S(2)}) collective-permute-start(bf16[128,2048]{1,0:T(8,128)(2,1)S(1)} %add_convert_fusion.1.refs_1_), channel_id=1, source_target_pairs={{0,2},{1,3},{2,0},{3,1},{4,6},{5,7},{6,4},{7,5},{8,10},{9,11},{10,... | collective-permute-start | bytes 1572872 | tf_op jit(solution)/shard_map/ppermute | solution.py:1136
  352.8 32.0 %collective-permute-start.28 = (bf16[4,256,512]{2,1,0:T(8,128)(2,1)}, bf16[4,256,512]{2,1,0:T(8,128)(2,1)}, u32[]{:S(2)}, u32[]{:S(2)}) collective-permute-start(bf16[4,256,512]{2,1,0:T(8,128)(2,1)} %grads_out_far.1), channel_id=1, source_target_pairs={{0,4},{4,0},{8,12},{12,8},{1,5},{5,1},{9,13},{13,9},{2,6},{6,2},{1... | collective-permute-start | bytes 3145736 | tf_op jit(solution)/shard_map/ppermute | solution.py:910
  352.8 14.7 %collective-permute-start.23 = (bf16[256,512]{1,0:T(8,128)(2,1)S(1)}, bf16[256,512]{1,0:T(8,128)(2,1)S(1)}, u32[]{:S(2)}, u32[]{:S(2)}) collective-permute-start(bf16[256,512]{1,0:T(8,128)(2,1)S(1)} %add_convert_fusion.5), channel_id=1, source_target_pairs={{0,8},{4,12},{8,0},{12,4},{1,9},{5,13},{9,1},{13,5},{2,10},{6,14},... | collective-permute-start | bytes 786440 | tf_op jit(solution)/shard_map/ppermute | solution.py:113
  352.9 19.0 %collective-permute-start.26 = (bf16[256,512]{1,0:T(8,128)(2,1)S(1)}, bf16[256,512]{1,0:T(8,128)(2,1)S(1)}, u32[]{:S(2)}, u32[]{:S(2)}) collective-permute-start(bf16[256,512]{1,0:T(8,128)(2,1)S(1)} %get-tuple-element.195), channel_id=1, source_target_pairs={{0,4},{4,0},{8,12},{12,8},{1,5},{5,1},{9,13},{13,9},{2,6},{6,2},{1... | collective-permute-start | bytes 786440 | tf_op jit(solution)/shard_map/ppermute | solution.py:112
  384.3 12.6 %collective-permute-start.27 = (bf16[128,2048]{1,0:T(8,128)(2,1)}, bf16[128,2048]{1,0:T(8,128)(2,1)}, u32[]{:S(2)}, u32[]{:S(2)}) collective-permute-start(bf16[128,2048]{1,0:T(8,128)(2,1)} %get-tuple-element.199), channel_id=1, source_target_pairs={{0,1},{1,0},{2,3},{3,2},{4,5},{5,4},{6,7},{7,6},{8,9},{9,8},{10,11... | collective-permute-start | bytes 1572872 | tf_op jit(solution)/shard_map/ppermute | solution.py:96
  396.9 22.6 %collective-permute-start.29 = (bf16[128,2048]{1,0:T(8,128)(2,1)S(1)}, bf16[128,2048]{1,0:T(8,128)(2,1)S(1)}, u32[]{:S(2)}, u32[]{:S(2)}) collective-permute-start(bf16[128,2048]{1,0:T(8,128)(2,1)S(1)} %copy-done.52), channel_id=1, source_target_pairs={{0,1},{1,0},{2,3},{3,2},{4,5},{5,4},{6,7},{7,6},{8,9},{9,8},{10,11... | collective-permute-start | bytes 1572872 | tf_op jit(solution)/shard_map/ppermute | solution.py:112
  399.8 24.8 %collective-permute-start.30 = (bf16[128,2048]{1,0:T(8,128)(2,1)S(1)}, bf16[128,2048]{1,0:T(8,128)(2,1)S(1)}, u32[]{:S(2)}, u32[]{:S(2)}) collective-permute-start(bf16[128,2048]{1,0:T(8,128)(2,1)S(1)} %add_convert_fusion), channel_id=1, source_target_pairs={{0,2},{1,3},{2,0},{3,1},{4,6},{5,7},{6,4},{7,5},{8,10},{9,11},{10,... | collective-permute-start | bytes 1572872 | tf_op jit(solution)/shard_map/ppermute | solution.py:113
  424.6 30.0 %collective-permute-start.34 = (bf16[2,256,512]{2,1,0:T(8,128)(2,1)}, bf16[2,256,512]{2,1,0:T(8,128)(2,1)}, u32[]{:S(2)}, u32[]{:S(2)}) collective-permute-start(bf16[2,256,512]{2,1,0:T(8,128)(2,1)} %get-tuple-element.218), channel_id=1, source_target_pairs={{0,8},{4,12},{8,0},{12,4},{1,9},{5,13},{9,1},{13,5},{2,10},{6,14},... | collective-permute-start | bytes 1572872 | tf_op jit(solution)/shard_map/ppermute | solution.py:914
  425.7 26.4 %collective-permute-start.32 = (bf16[128,2048]{1,0:T(8,128)(2,1)S(1)}, bf16[128,2048]{1,0:T(8,128)(2,1)}, u32[]{:S(2)}, u32[]{:S(2)}) collective-permute-start(bf16[128,2048]{1,0:T(8,128)(2,1)S(1)} %fusion.12.refs_1_), channel_id=1, source_target_pairs={{0,2},{1,3},{2,0},{3,1},{4,6},{5,7},{6,4},{7,5},{8,10},{9,11},{10,... | collective-permute-start | bytes 1572872 | tf_op jit(solution)/shard_map/ppermute | solution.py:1192
  425.8 26.5 %collective-permute-start.31 = (bf16[128,2048]{1,0:T(8,128)(2,1)S(1)}, bf16[128,2048]{1,0:T(8,128)(2,1)}, u32[]{:S(2)}, u32[]{:S(2)}) collective-permute-start(bf16[128,2048]{1,0:T(8,128)(2,1)S(1)} %fusion.12.refs_1_), channel_id=1, source_target_pairs={{0,1},{1,0},{2,3},{3,2},{4,5},{5,4},{6,7},{7,6},{8,9},{9,8},{10,11... | collective-permute-start | bytes 1572872 | tf_op jit(solution)/shard_map/ppermute | solution.py:1191
  433.4 25.1 %collective-permute-start.45 = (bf16[2,256,768]{2,1,0:T(8,128)(2,1)}, bf16[2,256,768]{2,1,0:T(8,128)(2,1)}, u32[]{:S(2)}, u32[]{:S(2)}) collective-permute-start(bf16[2,256,768]{2,1,0:T(8,128)(2,1)} %get-tuple-element.231), channel_id=1, source_target_pairs={{0,16},{16,0},{1,17},{17,1},{2,18},{18,2},{3,19},{19,3},{4,20},{20... | collective-permute-start | bytes 2359304 | tf_op jit(solution)/shard_map/ppermute | solution.py:918
  454.7 26.9 %collective-permute-start.36 = (bf16[128,2048]{1,0:T(8,128)(2,1)}, bf16[128,2048]{1,0:T(8,128)(2,1)S(1)}, u32[]{:S(2)}, u32[]{:S(2)}) collective-permute-start(bf16[128,2048]{1,0:T(8,128)(2,1)} %collective-permute-done.32.refs_3_), channel_id=1, source_target_pairs={{0,1},{1,0},{2,3},{3,2},{4,5},{5,4},{6,7},{7,6},{8,9},{9,8},{10,11... | collective-permute-start | bytes 1572872 | tf_op jit(solution)/shard_map/ppermute | solution.py:1198
  465.9 16.3 %collective-permute-start.33 = (bf16[128,2048]{1,0:T(8,128)(2,1)S(1)}, bf16[128,2048]{1,0:T(8,128)(2,1)S(1)}, u32[]{:S(2)}, u32[]{:S(2)}) collective-permute-start(bf16[128,2048]{1,0:T(8,128)(2,1)S(1)} %copy-done.43), channel_id=1, source_target_pairs={{0,1},{1,0},{2,3},{3,2},{4,5},{5,4},{6,7},{7,6},{8,9},{9,8},{10,11... | collective-permute-start | bytes 1572872 | tf_op jit(solution)/shard_map/ppermute | solution.py:1199
  (104 other events, 1114.1 us)
Sparse Core Ops, SparseCore 0:
  10.8 43.9 all-gather.2
  57.3 125.3 all-gather.4
  260.0 161.4 reduce-scatter.1

commit v2 on v1

--- a/solution.py
+++ b/solution.py
@@ -988,7 +988,7 @@
 def adamw_call(weight, first, second, terms, start, turned, step_rate, name, *deps):
     rows, columns = weight.shape
     long = rows if turned else columns
-    size = math.gcd(math.gcd(start, long), 512)
+    size = math.gcd(math.gcd(start, long), 1024)
     if turned:
         spec = pl.BlockSpec((size, columns), lambda j: (j, 0))
     else:

time: 498 us -> 497 us (level)
  waiting for transfers between devices: 202 us -> 186 us
  Pallas kernels: 164 us -> 171 us
  starting transfers between devices: 56 us -> 62.8 us
    ppermute x5, waiting for transfers between devices: 40.5 us -> 26.2 us  [scatter_middle(): lax.ppermute(near, axis, flip_pairs(count, 1))]
    ppermute x5, waiting for transfers between devices: 25.3 us -> 31.7 us  [scatter_middle(): lax.ppermute(joined, axis, flip_pairs(count, 2))]
    ppermute x5, waiting for transfers between devices: 19 us -> 25.1 us  [scatter_begin(): through = lax.ppermute(blocks[3].astype(LOW), axis, flip_pairs(count, 1))]
    pallas_call x2, Pallas kernels: 21.6 us -> 27.2 us  [attend_backward(): pl.pallas_call(with_deps(functools.partial(backward_kernel, devices, per_...]
    ppermute x2, starting transfers between devices: 0.07 us -> 5.23 us  [swap_along(): return lax.ppermute(values, 'dp', flip_pairs(2, 1))]
    ppermute x4, waiting for transfers between devices: 44 us -> 38.9 us  [gather_blocks(): far = lax.ppermute(rows, axis, flip_pairs(count, 2))]
  transfers between devices with their start and end apart: 50 -> 50, of which waited for: 29 -> 27; matrix products, arithmetic and copies ran while one was open for 7% -> 7% of each run, Pallas kernels for 25% -> 27%
where the time goes in v2:
time: 497 us; the launch traced here: 494 us
  waiting for transfers between devices  186 us (37%)
  Pallas kernels  171 us (34%)
  starting transfers between devices  62.8 us (13%)
  other arithmetic  27.9 us (6%)
  local copies, waits for them, and re-layouts  27.6 us (6%)
  between operations  14.8 us (3%)
    ppermute x4, waiting for transfers between devices, gather_blocks(): far = lax.ppermute(rows, axis, flip_pairs(count, 2))  38.9 us
    pallas_call x1, Pallas kernels, ffn_both(): tile_call(functools.partial(ffn_both_kernel, blocks, tiles), 'ffn_both',...  32.5 us
    ppermute x5, waiting for transfers between devices, scatter_middle(): lax.ppermute(joined, axis, flip_pairs(count, 2))  31.7 us
    pallas_call x2, Pallas kernels, attend_backward(): pl.pallas_call(with_deps(functools.partial(backward_kernel, devices, per_...  27.2 us
    ppermute x5, waiting for transfers between devices, scatter_middle(): lax.ppermute(near, axis, flip_pairs(count, 1))  26.2 us
    ppermute x5, waiting for transfers between devices, scatter_begin(): through = lax.ppermute(blocks[3].astype(LOW), axis, flip_pairs(count, 1))  25.1 us
    all_gather x1, waiting for transfers between devices, local(): full_small = lax.all_gather(small_shard, ('dp', 'ctx'), axis=0, tiled=True)  24.6 us
    unnamed x172, local copies, waits for them, and re-layouts  24.1 us
  transfers between devices with their start and end apart: 50, of which 27 were waited for; matrix products, arithmetic and copies ran while one was open for 7% of the time, Pallas kernels for 27%

profile of v2, /device:TPU:0, one launch (start us, length us, event | category | flops | bytes accessed | tf_op | source)
XLA Modules:
  0.0 494.1 jit_solution(5995193477204205707)
XLA Ops:
  30.2 24.6 %all-gather.3.cloned.1.call-done.refs_0_.refs_1_.refs_4_.refs_5_.refs_8_ = bf16[2048,1280]{1,0:T(8,128)(2,1)} async-done(((bf16[256,1280]{1,0:T(8,128)(2,1)}), bf16[2048,1280]{1,0:T(8,128)(2,1)}) %all-gather.3.cloned.1.call-update) | async-done | bytes 5242896 | tf_op jit(solution)/shard_map/all_gather | solution.py:1058
  54.8 3.7 fusion.3
  60.4 6.8 %collective-permute-done.5.refs_2_.refs_5_ = bf16[2,128,512]{2,1,0:T(8,128)(2,1)S(1)} collective-permute-done((bf16[2,128,512]{2,1,0:T(8,128)(2,1)S(1)}, bf16[2,128,512]{2,1,0:T(8,128)(2,1)S(1)}, u32[]{:S(2)}, u32[]{:S(2)}) %collective-permute-start.5) | collective-permute-done | bytes 262176 | tf_op jit(solution)/shard_map/ppermute | solution.py:167
  68.8 18.7 %attend_forward.1 = (f32[2,4,64,512]{3,2,1,0:T(8,128)S(1)}, bf16[2,4,64,512]{3,2,1,0:T(8,128)(2,1)S(1)}, f32[2,4,1,512]{3,2,1,0:T(1,128)S(1)}) custom-call(s32[8]{0:T(128)S(1)} %select_reduce_fusion.order_ref.refs_0_, s32[2]{0:T(128)S(1)} %and_select_fusion.rank_ref.refs_1_, s32[4]{0:T(128)S(1)} %pad_add_fusion.1.peer_ref.refs_2_, ...), custom_call_target="tpu_custom_call" | custom-call | flops 34359738368 | bytes 8388608 | tf_op jit(solution)/shard_map/attend_forward/pallas_call | solution.py:347
  89.2 7.4 %project_out.1 = (f32[128,2048]{1,0:T(8,128)S(1)}, bf16[128,2048]{1,0:T(8,128)(2,1)}, f32[128,2048]{1,0:T(8,128)S(1)}, bf16[128,2048]{1,0:T(8,128)(2,1)S(1)}, bf16[512,512]{1,0:T(8,128)(2,1)S(1)}) custom-call(s32[4]{0:T(128)S(1)} %pad_add_fusion.peer_ref.refs_0_, bf16[512,512]{1,0:T(8,128)(2,1)S(1)} %bitcast.82, ...), custom_call_target="tpu_custom_call" | custom-call | flops 1610612736 | bytes 4194304 | tf_op jit(solution)/shard_map/project_out/pallas_call | solution.py:821
  98.9 18.7 %collective-permute-done.7 = bf16[128,2048]{1,0:T(8,128)(2,1)S(1)} collective-permute-done((bf16[128,2048]{1,0:T(8,128)(2,1)S(1)}, bf16[128,2048]{1,0:T(8,128)(2,1)S(1)}, u32[]{:S(2)}, u32[]{:S(2)}) %collective-permute-start.7) | collective-permute-done | bytes 524320 | tf_op jit(solution)/shard_map/ppermute | solution.py:96
  118.4 3.9 collective-permute-start.9
  122.3 11.6 %collective-permute-done.8 = bf16[128,2048]{1,0:T(8,128)(2,1)} collective-permute-done((bf16[128,2048]{1,0:T(8,128)(2,1)}, bf16[128,2048]{1,0:T(8,128)(2,1)}, u32[]{:S(2)}, u32[]{:S(2)}) %collective-permute-start.8) | collective-permute-done | bytes 524320 | tf_op jit(solution)/shard_map/ppermute | solution.py:112
  133.9 12.1 %collective-permute-done.9 = bf16[128,2048]{1,0:T(8,128)(2,1)} collective-permute-done((bf16[128,2048]{1,0:T(8,128)(2,1)}, bf16[128,2048]{1,0:T(8,128)(2,1)}, u32[]{:S(2)}, u32[]{:S(2)}) %collective-permute-start.9) | collective-permute-done | bytes 524320 | tf_op jit(solution)/shard_map/ppermute | solution.py:113
  151.8 13.2 %collective-permute-done.11.refs_2_ = bf16[128,2048]{1,0:T(8,128)(2,1)S(1)} collective-permute-done((bf16[128,2048]{1,0:T(8,128)(2,1)S(1)}, bf16[128,2048]{1,0:T(8,128)(2,1)S(1)}, u32[]{:S(2)}, u32[]{:S(2)}) %collective-permute-start.11) | collective-permute-done | bytes 524320 | tf_op jit(solution)/shard_map/ppermute | solution.py:167
  169.7 5.5 %collective-permute-done.12.refs_3_ = bf16[128,2048]{1,0:T(8,128)(2,1)S(1)} collective-permute-done((bf16[128,2048]{1,0:T(8,128)(2,1)S(1)}, bf16[128,2048]{1,0:T(8,128)(2,1)S(1)}, u32[]{:S(2)}, u32[]{:S(2)}) %collective-permute-start.12) | collective-permute-done | bytes 524320 | tf_op jit(solution)/shard_map/ppermute | solution.py:169
  176.0 6.6 %all-gather.5.cloned.1.call-done.refs_5_.refs_6_.refs_7_.refs_8_.refs_9_.refs_1_ = bf16[2048,6144]{1,0:T(8,128)(2,1)} async-done(((bf16[256,6144]{1,0:T(8,128)(2,1)}), bf16[2048,6144]{1,0:T(8,128)(2,1)}) %all-gather.5.cloned.1.call-update) | async-done | bytes 25165840 | tf_op jit(solution)/shard_map/all_gather | solution.py:1061
  185.7 32.5 %ffn_both.1 = (bf16[512,2048]{1,0:T(8,128)(2,1)}, bf16[512,2048]{1,0:T(8,128)(2,1)}, bf16[512,2048]{1,0:T(8,128)(2,1)}, f32[128,2048]{1,0:T(8,128)S(1)}, bf16[12...) custom-call(bf16[128,2048]{1,0:T(8,128)(2,1)S(1)} %copy-done.19, ...), custom_call_target="tpu_custom_call" | custom-call | flops 32212254720 | bytes 18874368 | tf_op jit(solution)/shard_map/ffn_both/pallas_call | solution.py:560
  219.7 9.8 %ffn_out.1 = (f32[128,2048]{1,0:T(8,128)S(1)}, bf16[128,2048]{1,0:T(8,128)(2,1)S(1)}, f32[128,2048]{1,0:T(8,128)S(1)}, bf16[128,2048]{1,0:T(8,128)(2,1)S(1)}) custom-call(bf16[512,2048]{1,0:T(8,128)(2,1)} %get-tuple-element.147.refs_0_.refs_5_, bf16[2048,6144]{1,0:T(8,128)(2,1)} %all-gather.5.cloned.1.call-done.refs_5_.refs_6_.refs_7_.refs_8_.refs_9_.refs_1_, ...), custom_call_target="tpu_custom_call" | custom-call | flops 6442450944 | bytes 6291456 | tf_op jit(solution)/shard_map/ffn_out/pallas_call | solution.py:584
  236.4 19.8 %ffn_grads.1 = (bf16[2048,6144]{1,0:T(8,128)(2,1)}, f32[8,128]{1,0:T(8,128)}) custom-call(bf16[128,2048]{1,0:T(8,128)(2,1)S(1)} %copy-done.19, bf16[128,2048]{1,0:T(8,128)(2,1)} %collective-permute-done.10.refs_1_, bf16[128,2048]{1,0:T(8,128)(2,1)S(1)} %copy-done.36, bf16[128,2048]{1,0:T(8,128)(2,1)S(1)} %copy-done.39, bf16[512,2048]{1,0:T(8,128)(2,1)S(1)} %copy-done.2, ...), custom_call_target="tpu_custom_call" | custom-call | flops 19327352832 | bytes 50339840 | tf_op jit(solution)/shard_map/ffn_grads/pallas_call | solution.py:611
  268.9 18.9 %collective-permute-done.17.refs_2_.refs_3_ = bf16[128,2048]{1,0:T(8,128)(2,1)S(1)} collective-permute-done((bf16[128,2048]{1,0:T(8,128)(2,1)S(1)}, bf16[128,2048]{1,0:T(8,128)(2,1)S(1)}, u32[]{:S(2)}, u32[]{:S(2)}) %collective-permute-start.17) | collective-permute-done | bytes 524320 | tf_op jit(solution)/shard_map/ppermute | solution.py:167
  288.9 11.4 %collective-permute-done.18.refs_3_.refs_13_.refs_17_.refs_4_ = bf16[128,2048]{1,0:T(8,128)(2,1)} collective-permute-done((bf16[128,2048]{1,0:T(8,128)(2,1)S(1)}, bf16[128,2048]{1,0:T(8,128)(2,1)}, u32[]{:S(2)}, u32[]{:S(2)}) %collective-permute-start.18) | collective-permute-done | bytes 524320 | tf_op jit(solution)/shard_map/ppermute | solution.py:169
  302.0 5.0 %mix_back.1 = bf16[512,512]{1,0:T(8,128)(2,1)S(1)} custom-call(s32[4]{0:T(128)S(1)} %pad_add_fusion.peer_ref.refs_0_, bf16[128,2048]{1,0:T(8,128)(2,1)S(1)} %copy-done.4, bf16[128,2048]{1,0:T(8,128)(2,1)S(1)} %collective-permute-done.16.refs_1_.refs_2_, bf16[128,2048]{1,0:T(8,128)(2,1)S(1)} %collective-permute-done.17.refs_2_.refs_3_, ...), custom_call_target="tpu_custom_call" | custom-call | flops 1610612736 | bytes 4194304 | tf_op jit(solution)/shard_map/mix_back/pallas_call | solution.py:882
  307.1 13.7 %attend_backward.2 = (bf16[1,4,64,512]{3,2,1,0:T(8,128)(2,1)S(1)}, bf16[128,512]{1,0:T(8,128)(2,1)S(1)}, bf16[128,512]{1,0:T(8,128)(2,1)S(1)}, bf16[128,512]{1,0:T(8,128)(2,1)S(1)}, bf16[128,512]{1,0:T(8,128)(2,1)S(1)}) custom-call(s32[8]{0:T(128)S(1)} %select_reduce_fusion.order_ref.refs_0_, s32[2]{0:T(128)S(1)} %and_select_fusion.rank_ref.refs_1_, ...), custom_call_target="tpu_custom_call" | custom-call | flops 34359738368 | bytes 8388608 | tf_op jit(solution)/shard_map/attend_backward/pallas_call | solution.py:397
  325.3 13.5 %attend_backward.3 = (bf16[1,4,64,512]{3,2,1,0:T(8,128)(2,1)S(1)}, bf16[256,512]{1,0:T(8,128)(2,1)S(1)}, bf16[256,512]{1,0:T(8,128)(2,1)S(1)}, bf16[256,512]{1,0:T(8,128)(2,1)S(1)}, bf16[256,512]{1,0:T(8,128)(2,1)S(1)}) custom-call(s32[8]{0:T(128)S(1)} %select_reduce_fusion.order_ref.refs_0_, s32[2]{0:T(128)S(1)} %and_select_fusion.rank_ref.refs_1_, ...), custom_call_target="tpu_custom_call" | custom-call | flops 34359738368 | bytes 8388608 | tf_op jit(solution)/shard_map/attend_backward/pallas_call | solution.py:397
  339.2 3.5 collective-permute-start.25
  345.6 4.4 grads_out_far.1
  352.6 12.4 %collective-permute-done.23.refs_5_ = bf16[256,512]{1,0:T(8,128)(2,1)S(1)} collective-permute-done((bf16[256,512]{1,0:T(8,128)(2,1)S(1)}, bf16[256,512]{1,0:T(8,128)(2,1)S(1)}, u32[]{:S(2)}, u32[]{:S(2)}) %collective-permute-start.23) | collective-permute-done | bytes 262176 | tf_op jit(solution)/shard_map/ppermute | solution.py:113
  369.9 8.0 %project_back.1 = (f32[128,2048]{1,0:T(8,128)S(1)}, bf16[128,2048]{1,0:T(8,128)(2,1)S(1)}, f32[128,2048]{1,0:T(8,128)S(1)}, bf16[128,2048]{1,0:T(8,128)(2,1)}, bf16[768,512]{1,0:T(8,128)(2,1)S(1)}) custom-call(s32[4]{0:T(128)S(1)} %pad_add_fusion.peer_ref.refs_0_, bf16[256,512]{1,0:T(8,128)(2,1)S(1)} %bitcast.83, bf16[256,512]{1,0:T(8,128)(2,1)S(1)} %bitcast.84, ...), custom_call_target="tpu_custom_call" | custom-call | flops 1000 | bytes 1000 | tf_op jit(solution)/shard_map/project_back/pallas_call | solution.py:733
  384.2 4.6 grads_out_near.1
  388.8 5.4 %collective-permute-done.27 = bf16[128,2048]{1,0:T(8,128)(2,1)} collective-permute-done((bf16[128,2048]{1,0:T(8,128)(2,1)}, bf16[128,2048]{1,0:T(8,128)(2,1)}, u32[]{:S(2)}, u32[]{:S(2)}) %collective-permute-start.27) | collective-permute-done | bytes 524320 | tf_op jit(solution)/shard_map/ppermute | solution.py:96
  402.3 14.4 %collective-permute-done.29 = bf16[128,2048]{1,0:T(8,128)(2,1)S(1)} collective-permute-done((bf16[128,2048]{1,0:T(8,128)(2,1)S(1)}, bf16[128,2048]{1,0:T(8,128)(2,1)S(1)}, u32[]{:S(2)}, u32[]{:S(2)}) %collective-permute-start.29) | collective-permute-done | bytes 524320 | tf_op jit(solution)/shard_map/ppermute | solution.py:112
  416.8 5.1 %collective-permute-done.30 = bf16[128,2048]{1,0:T(8,128)(2,1)S(1)} collective-permute-done((bf16[128,2048]{1,0:T(8,128)(2,1)S(1)}, bf16[128,2048]{1,0:T(8,128)(2,1)S(1)}, u32[]{:S(2)}, u32[]{:S(2)}) %collective-permute-start.30) | collective-permute-done | bytes 524320 | tf_op jit(solution)/shard_map/ppermute | solution.py:113
  426.5 4.6 grads_qkv_near.1
  436.2 10.1 %adamw_gate_up.1 = (f32[256,4096]{1,0:T(8,128)}, f32[256,4096]{1,0:T(8,128)}, f32[256,4096]{1,0:T(8,128)}, f32[8,128]{1,0:T(8,128)S(1)}) custom-call(f32[256,4096]{1,0:T(8,128)} %refs_0_.4, f32[256,4096]{1,0:T(8,128)} %refs_1_.4, f32[256,4096]{1,0:T(8,128)} %refs_2_.4, bf16[256,6144]{1,0:T(8,128)(2,1)S(1)} %copy-done.1, ...), custom_call_target="tpu_custom_call" | custom-call | flops 31457280 | bytes 25174016 | tf_op jit(solution)/shard_map/adamw_gate_up/pallas_call | solution.py:999
  468.6 5.1 %adamw_down.1 = (f32[2048,256]{1,0:T(8,128)}, f32[2048,256]{1,0:T(8,128)}, f32[2048,256]{1,0:T(8,128)}, f32[8,128]{1,0:T(8,128)S(1)}) custom-call(f32[2048,256]{1,0:T(8,128)S(1)} %copy-done.7, f32[2048,256]{1,0:T(8,128)S(1)} %copy-done.26, f32[2048,256]{1,0:T(8,128)} %refs_2_.5, bf16[256,6144]{1,0:T(8,128)(2,1)} %reduce-scatter.2.cloned.1.call-done.refs_3_, ...), custom_call_target="tpu_custom_call" | custom-call | flops 15728640 | bytes 12591104 | tf_op jit(solution)/shard_map/adamw_down/pallas_call | solution.py:999
  483.4 4.2 place_rows.3
  (334 shorter events, 140.1 us)
Async XLA Ops:
  7.2 47.6 %all-gather.3.cloned.1.call-start = ((), (), s32[]{:S(2)}) async-start(), calls=%async_computation.1 | async-start | bytes 5898240 | tf_op jit(solution)/shard_map/all_gather | solution.py:1058
  10.7 172.0 %all-gather.5.cloned.1.call-start = ((), (), s32[]{:S(2)}) async-start(), calls=%async_computation.2 | async-start | bytes 28311552 | tf_op jit(solution)/shard_map/all_gather | solution.py:1061
  15.7 418.6 %reduce-scatter.2.cloned.1.call-start = ((), (), s32[]{:S(2)}) async-start(), calls=%async_computation.3 | async-start | bytes 28311552 | tf_op jit(solution)/shard_map/reduce_scatter | solution.py:1108
  97.4 20.2 %collective-permute-start.7 = (bf16[128,2048]{1,0:T(8,128)(2,1)S(1)}, bf16[128,2048]{1,0:T(8,128)(2,1)S(1)}, u32[]{:S(2)}, u32[]{:S(2)}) collective-permute-start(bf16[128,2048]{1,0:T(8,128)(2,1)S(1)} %get-tuple-element.138), channel_id=1, source_target_pairs={{0,1},{1,0},{2,3},{3,2},{4,5},{5,4},{6,7},{7,6},{8,9},{9,8},{10,11... | collective-permute-start | bytes 1572872 | tf_op jit(solution)/shard_map/ppermute | solution.py:96
  117.5 16.4 %collective-permute-start.8 = (bf16[128,2048]{1,0:T(8,128)(2,1)}, bf16[128,2048]{1,0:T(8,128)(2,1)}, u32[]{:S(2)}, u32[]{:S(2)}) collective-permute-start(bf16[128,2048]{1,0:T(8,128)(2,1)} %get-tuple-element.139), channel_id=1, source_target_pairs={{0,1},{1,0},{2,3},{3,2},{4,5},{5,4},{6,7},{7,6},{8,9},{9,8},{10,11... | collective-permute-start | bytes 1572872 | tf_op jit(solution)/shard_map/ppermute | solution.py:112
  118.4 27.6 %collective-permute-start.9 = (bf16[128,2048]{1,0:T(8,128)(2,1)}, bf16[128,2048]{1,0:T(8,128)(2,1)}, u32[]{:S(2)}, u32[]{:S(2)}) collective-permute-start(bf16[128,2048]{1,0:T(8,128)(2,1)} %add_convert_fusion.4), channel_id=1, source_target_pairs={{0,2},{1,3},{2,0},{3,1},{4,6},{5,7},{6,4},{7,5},{8,10},{9,11},{10,... | collective-permute-start | bytes 1572872 | tf_op jit(solution)/shard_map/ppermute | solution.py:113
  149.8 15.1 %collective-permute-start.11 = (bf16[128,2048]{1,0:T(8,128)(2,1)S(1)}, bf16[128,2048]{1,0:T(8,128)(2,1)S(1)}, u32[]{:S(2)}, u32[]{:S(2)}) collective-permute-start(bf16[128,2048]{1,0:T(8,128)(2,1)S(1)} %multiply_convert_fusion.refs_0_), channel_id=1, source_target_pairs={{0,2},{1,3},{2,0},{3,1},{4,6},{5,7},{6,4},{7,5},{8,10},{9,11},{10,... | collective-permute-start | bytes 1572872 | tf_op jit(solution)/shard_map/ppermute | solution.py:167
  149.9 16.1 %collective-permute-start.10 = (bf16[128,2048]{1,0:T(8,128)(2,1)S(1)}, bf16[128,2048]{1,0:T(8,128)(2,1)}, u32[]{:S(2)}, u32[]{:S(2)}) collective-permute-start(bf16[128,2048]{1,0:T(8,128)(2,1)S(1)} %multiply_convert_fusion.refs_0_), channel_id=1, source_target_pairs={{0,1},{1,0},{2,3},{3,2},{4,5},{5,4},{6,7},{7,6},{8,9},{9,8},{10,11... | collective-permute-start | bytes 1572872 | tf_op jit(solution)/shard_map/ppermute | solution.py:166
  218.2 14.1 %collective-permute-start.13 = (bf16[128,2048]{1,0:T(8,128)(2,1)S(1)}, bf16[128,2048]{1,0:T(8,128)(2,1)S(1)}, u32[]{:S(2)}, u32[]{:S(2)}) collective-permute-start(bf16[128,2048]{1,0:T(8,128)(2,1)S(1)} %get-tuple-element.146), channel_id=1, source_target_pairs={{0,1},{1,0},{2,3},{3,2},{4,5},{5,4},{6,7},{7,6},{8,9},{9,8},{10,11... | collective-permute-start | bytes 1572872 | tf_op jit(solution)/shard_map/ppermute | solution.py:96
  232.3 24.1 %collective-permute-start.14 = (bf16[128,2048]{1,0:T(8,128)(2,1)S(1)}, bf16[128,2048]{1,0:T(8,128)(2,1)S(1)}, u32[]{:S(2)}, u32[]{:S(2)}) collective-permute-start(bf16[128,2048]{1,0:T(8,128)(2,1)S(1)} %get-tuple-element.150), channel_id=1, source_target_pairs={{0,1},{1,0},{2,3},{3,2},{4,5},{5,4},{6,7},{7,6},{8,9},{9,8},{10,11... | collective-permute-start | bytes 1572872 | tf_op jit(solution)/shard_map/ppermute | solution.py:112
  233.9 25.3 %collective-permute-start.15 = (bf16[128,2048]{1,0:T(8,128)(2,1)S(1)}, bf16[128,2048]{1,0:T(8,128)(2,1)}, u32[]{:S(2)}, u32[]{:S(2)}) collective-permute-start(bf16[128,2048]{1,0:T(8,128)(2,1)S(1)} %add_convert_fusion.3), channel_id=1, source_target_pairs={{0,2},{1,3},{2,0},{3,1},{4,6},{5,7},{6,4},{7,5},{8,10},{9,11},{10,... | collective-permute-start | bytes 1572872 | tf_op jit(solution)/shard_map/ppermute | solution.py:113
  265.2 22.6 %collective-permute-start.17 = (bf16[128,2048]{1,0:T(8,128)(2,1)S(1)}, bf16[128,2048]{1,0:T(8,128)(2,1)S(1)}, u32[]{:S(2)}, u32[]{:S(2)}) collective-permute-start(bf16[128,2048]{1,0:T(8,128)(2,1)S(1)} %get-tuple-element.253.refs_0_.refs_1_), channel_id=1, source_target_pairs={{0,2},{1,3},{2,0},{3,1},{4,6},{5,7},{6,4},{7,5},{8,10},{9,11},{10,... | collective-permute-start | bytes 1572872 | tf_op jit(solution)/shard_map/ppermute | solution.py:167
  265.3 22.5 %collective-permute-start.16 = (bf16[128,2048]{1,0:T(8,128)(2,1)S(1)}, bf16[128,2048]{1,0:T(8,128)(2,1)S(1)}, u32[]{:S(2)}, u32[]{:S(2)}) collective-permute-start(bf16[128,2048]{1,0:T(8,128)(2,1)S(1)} %get-tuple-element.253.refs_0_.refs_1_), channel_id=1, source_target_pairs={{0,1},{1,0},{2,3},{3,2},{4,5},{5,4},{6,7},{7,6},{8,9},{9,8},{10,11... | collective-permute-start | bytes 1572872 | tf_op jit(solution)/shard_map/ppermute | solution.py:166
  287.8 12.5 %collective-permute-start.18 = (bf16[128,2048]{1,0:T(8,128)(2,1)S(1)}, bf16[128,2048]{1,0:T(8,128)(2,1)}, u32[]{:S(2)}, u32[]{:S(2)}) collective-permute-start(bf16[128,2048]{1,0:T(8,128)(2,1)S(1)} %collective-permute-done.17.refs_2_.refs_3_), channel_id=1, source_target_pairs={{0,1},{1,0},{2,3},{3,2},{4,5},{5,4},{6,7},{7,6},{8,9},{9,8},{10,11... | collective-permute-start | bytes 1572872 | tf_op jit(solution)/shard_map/ppermute | solution.py:169
  300.3 20.6 %collective-permute-start.19 = (bf16[128,2048]{1,0:T(8,128)(2,1)}, bf16[128,2048]{1,0:T(8,128)(2,1)S(1)}, u32[]{:S(2)}, u32[]{:S(2)}) collective-permute-start(bf16[128,2048]{1,0:T(8,128)(2,1)} %copy-done.50), channel_id=1, source_target_pairs={{0,1},{1,0},{2,3},{3,2},{4,5},{5,4},{6,7},{7,6},{8,9},{9,8},{10,11... | collective-permute-start | bytes 1572872 | tf_op jit(solution)/shard_map/ppermute | solution.py:96
  320.9 17.9 %collective-permute-start.20 = (bf16[128,2048]{1,0:T(8,128)(2,1)S(1)}, bf16[128,2048]{1,0:T(8,128)(2,1)S(1)}, u32[]{:S(2)}, u32[]{:S(2)}) collective-permute-start(bf16[128,2048]{1,0:T(8,128)(2,1)S(1)} %copy-done.49), channel_id=1, source_target_pairs={{0,1},{1,0},{2,3},{3,2},{4,5},{5,4},{6,7},{7,6},{8,9},{9,8},{10,11... | collective-permute-start | bytes 1572872 | tf_op jit(solution)/shard_map/ppermute | solution.py:112
  322.8 16.0 %collective-permute-start.21 = (bf16[128,2048]{1,0:T(8,128)(2,1)S(1)}, bf16[128,2048]{1,0:T(8,128)(2,1)S(1)}, u32[]{:S(2)}, u32[]{:S(2)}) collective-permute-start(bf16[128,2048]{1,0:T(8,128)(2,1)S(1)} %add_convert_fusion.2), channel_id=1, source_target_pairs={{0,2},{1,3},{2,0},{3,1},{4,6},{5,7},{6,4},{7,5},{8,10},{9,11},{10,... | collective-permute-start | bytes 1572872 | tf_op jit(solution)/shard_map/ppermute | solution.py:113
  339.2 27.1 %collective-permute-start.25 = (bf16[128,2048]{1,0:T(8,128)(2,1)S(1)}, bf16[128,2048]{1,0:T(8,128)(2,1)S(1)}, u32[]{:S(2)}, u32[]{:S(2)}) collective-permute-start(bf16[128,2048]{1,0:T(8,128)(2,1)S(1)} %add_convert_fusion.1.refs_1_), channel_id=1, source_target_pairs={{0,1},{1,0},{2,3},{3,2},{4,5},{5,4},{6,7},{7,6},{8,9},{9,8},{10,11... | collective-permute-start | bytes 1572872 | tf_op jit(solution)/shard_map/ppermute | solution.py:1137
  342.6 26.5 %collective-permute-start.24 = (bf16[128,2048]{1,0:T(8,128)(2,1)S(1)}, bf16[128,2048]{1,0:T(8,128)(2,1)S(1)}, u32[]{:S(2)}, u32[]{:S(2)}) collective-permute-start(bf16[128,2048]{1,0:T(8,128)(2,1)S(1)} %add_convert_fusion.1.refs_1_), channel_id=1, source_target_pairs={{0,2},{1,3},{2,0},{3,1},{4,6},{5,7},{6,4},{7,5},{8,10},{9,11},{10,... | collective-permute-start | bytes 1572872 | tf_op jit(solution)/shard_map/ppermute | solution.py:1136
  350.0 32.0 %collective-permute-start.28 = (bf16[4,256,512]{2,1,0:T(8,128)(2,1)}, bf16[4,256,512]{2,1,0:T(8,128)(2,1)}, u32[]{:S(2)}, u32[]{:S(2)}) collective-permute-start(bf16[4,256,512]{2,1,0:T(8,128)(2,1)} %grads_out_far.1), channel_id=1, source_target_pairs={{0,4},{4,0},{8,12},{12,8},{1,5},{5,1},{9,13},{13,9},{2,6},{6,2},{1... | collective-permute-start | bytes 3145736 | tf_op jit(solution)/shard_map/ppermute | solution.py:910
  350.1 14.9 %collective-permute-start.23 = (bf16[256,512]{1,0:T(8,128)(2,1)S(1)}, bf16[256,512]{1,0:T(8,128)(2,1)S(1)}, u32[]{:S(2)}, u32[]{:S(2)}) collective-permute-start(bf16[256,512]{1,0:T(8,128)(2,1)S(1)} %add_convert_fusion.5), channel_id=1, source_target_pairs={{0,8},{4,12},{8,0},{12,4},{1,9},{5,13},{9,1},{13,5},{2,10},{6,14},... | collective-permute-start | bytes 786440 | tf_op jit(solution)/shard_map/ppermute | solution.py:113
  352.3 16.8 %collective-permute-start.26 = (bf16[256,512]{1,0:T(8,128)(2,1)S(1)}, bf16[256,512]{1,0:T(8,128)(2,1)S(1)}, u32[]{:S(2)}, u32[]{:S(2)}) collective-permute-start(bf16[256,512]{1,0:T(8,128)(2,1)S(1)} %get-tuple-element.195), channel_id=1, source_target_pairs={{0,4},{4,0},{8,12},{12,8},{1,5},{5,1},{9,13},{13,9},{2,6},{6,2},{1... | collective-permute-start | bytes 786440 | tf_op jit(solution)/shard_map/ppermute | solution.py:112
  381.5 12.6 %collective-permute-start.27 = (bf16[128,2048]{1,0:T(8,128)(2,1)}, bf16[128,2048]{1,0:T(8,128)(2,1)}, u32[]{:S(2)}, u32[]{:S(2)}) collective-permute-start(bf16[128,2048]{1,0:T(8,128)(2,1)} %get-tuple-element.199), channel_id=1, source_target_pairs={{0,1},{1,0},{2,3},{3,2},{4,5},{5,4},{6,7},{7,6},{8,9},{9,8},{10,11... | collective-permute-start | bytes 1572872 | tf_op jit(solution)/shard_map/ppermute | solution.py:96
  394.2 22.6 %collective-permute-start.29 = (bf16[128,2048]{1,0:T(8,128)(2,1)S(1)}, bf16[128,2048]{1,0:T(8,128)(2,1)S(1)}, u32[]{:S(2)}, u32[]{:S(2)}) collective-permute-start(bf16[128,2048]{1,0:T(8,128)(2,1)S(1)} %copy-done.52), channel_id=1, source_target_pairs={{0,1},{1,0},{2,3},{3,2},{4,5},{5,4},{6,7},{7,6},{8,9},{9,8},{10,11... | collective-permute-start | bytes 1572872 | tf_op jit(solution)/shard_map/ppermute | solution.py:112
  397.2 24.7 %collective-permute-start.30 = (bf16[128,2048]{1,0:T(8,128)(2,1)S(1)}, bf16[128,2048]{1,0:T(8,128)(2,1)S(1)}, u32[]{:S(2)}, u32[]{:S(2)}) collective-permute-start(bf16[128,2048]{1,0:T(8,128)(2,1)S(1)} %add_convert_fusion), channel_id=1, source_target_pairs={{0,2},{1,3},{2,0},{3,1},{4,6},{5,7},{6,4},{7,5},{8,10},{9,11},{10,... | collective-permute-start | bytes 1572872 | tf_op jit(solution)/shard_map/ppermute | solution.py:113
  421.9 30.2 %collective-permute-start.34 = (bf16[2,256,512]{2,1,0:T(8,128)(2,1)}, bf16[2,256,512]{2,1,0:T(8,128)(2,1)}, u32[]{:S(2)}, u32[]{:S(2)}) collective-permute-start(bf16[2,256,512]{2,1,0:T(8,128)(2,1)} %get-tuple-element.218), channel_id=1, source_target_pairs={{0,8},{4,12},{8,0},{12,4},{1,9},{5,13},{9,1},{13,5},{2,10},{6,14},... | collective-permute-start | bytes 1572872 | tf_op jit(solution)/shard_map/ppermute | solution.py:914
  423.7 25.9 %collective-permute-start.32 = (bf16[128,2048]{1,0:T(8,128)(2,1)S(1)}, bf16[128,2048]{1,0:T(8,128)(2,1)}, u32[]{:S(2)}, u32[]{:S(2)}) collective-permute-start(bf16[128,2048]{1,0:T(8,128)(2,1)S(1)} %fusion.12.refs_1_), channel_id=1, source_target_pairs={{0,2},{1,3},{2,0},{3,1},{4,6},{5,7},{6,4},{7,5},{8,10},{9,11},{10,... | collective-permute-start | bytes 1572872 | tf_op jit(solution)/shard_map/ppermute | solution.py:1192
  423.7 26.0 %collective-permute-start.31 = (bf16[128,2048]{1,0:T(8,128)(2,1)S(1)}, bf16[128,2048]{1,0:T(8,128)(2,1)}, u32[]{:S(2)}, u32[]{:S(2)}) collective-permute-start(bf16[128,2048]{1,0:T(8,128)(2,1)S(1)} %fusion.12.refs_1_), channel_id=1, source_target_pairs={{0,1},{1,0},{2,3},{3,2},{4,5},{5,4},{6,7},{7,6},{8,9},{9,8},{10,11... | collective-permute-start | bytes 1572872 | tf_op jit(solution)/shard_map/ppermute | solution.py:1191
  431.1 25.0 %collective-permute-start.45 = (bf16[2,256,768]{2,1,0:T(8,128)(2,1)}, bf16[2,256,768]{2,1,0:T(8,128)(2,1)}, u32[]{:S(2)}, u32[]{:S(2)}) collective-permute-start(bf16[2,256,768]{2,1,0:T(8,128)(2,1)} %get-tuple-element.231), channel_id=1, source_target_pairs={{0,16},{16,0},{1,17},{17,1},{2,18},{18,2},{3,19},{19,3},{4,20},{20... | collective-permute-start | bytes 2359304 | tf_op jit(solution)/shard_map/ppermute | solution.py:918
  452.1 28.2 %collective-permute-start.36 = (bf16[128,2048]{1,0:T(8,128)(2,1)}, bf16[128,2048]{1,0:T(8,128)(2,1)S(1)}, u32[]{:S(2)}, u32[]{:S(2)}) collective-permute-start(bf16[128,2048]{1,0:T(8,128)(2,1)} %collective-permute-done.32.refs_3_), channel_id=1, source_target_pairs={{0,1},{1,0},{2,3},{3,2},{4,5},{5,4},{6,7},{7,6},{8,9},{9,8},{10,11... | collective-permute-start | bytes 1572872 | tf_op jit(solution)/shard_map/ppermute | solution.py:1198
  464.3 12.0 %collective-permute-start.44 = (bf16[256,512]{1,0:T(8,128)(2,1)S(1)}, bf16[256,512]{1,0:T(8,128)(2,1)S(1)}, u32[]{:S(2)}, u32[]{:S(2)}) collective-permute-start(bf16[256,512]{1,0:T(8,128)(2,1)S(1)} %fusion.17), channel_id=1, source_target_pairs={{0,16},{16,0},{1,17},{17,1},{2,18},{18,2},{3,19},{19,3},{4,20},{20... | collective-permute-start | bytes 786440 | tf_op jit(solution)/shard_map/ppermute | solution.py:918
  466.4 14.5 %collective-permute-start.33 = (bf16[128,2048]{1,0:T(8,128)(2,1)S(1)}, bf16[128,2048]{1,0:T(8,128)(2,1)S(1)}, u32[]{:S(2)}, u32[]{:S(2)}) collective-permute-start(bf16[128,2048]{1,0:T(8,128)(2,1)S(1)} %copy-done.43), channel_id=1, source_target_pairs={{0,1},{1,0},{2,3},{3,2},{4,5},{5,4},{6,7},{7,6},{8,9},{9,8},{10,11... | collective-permute-start | bytes 1572872 | tf_op jit(solution)/shard_map/ppermute | solution.py:1199
  (104 other events, 1096.5 us)
Sparse Core Ops, SparseCore 0:
  10.8 43.9 all-gather.2
  57.3 125.3 all-gather.4
  260.0 161.4 reduce-scatter.1
